TPU v7x, 32 devices: a whole 2x2x4 slice. The times are simulated.
32 devices in a mesh: blk: 16 (over z, y, core), rhs: 2 (over x).
Axes of the slice: x: 2, y: 2, z: 4, core: 2. Of those that a mesh axis runs over, the one named last changes fastest.
Arguments:
- positions: float32 [3, 4096], P(None, 'blk'), may hold values from -1 to 1
- normal_angles: float32 [2, 4096], P(None, 'blk'), may hold values from -3.140625 to 3.140625
- areas: float32 [4096], P('blk'), may hold values from 1 to 6
- densities: float32 [2, 2, 4096], P('rhs', None, 'blk'), may hold values from -6 to 6
- need_owner: int32 [4096, 1], P('blk'), may hold values from 0 to 15; in each aligned block of 256 rows (0 to 255, 256 to 511, ...) at most 64 rows name the same one
- need_slot: int32 [4096], P('blk'), may hold values from 0 to 255
- near_index: int32 [32, 4096], P(None, 'blk'), may hold values from 0 to 255
- near_coef: float32 [2, 32, 4096], P(None, None, 'blk'), may hold values from -2 to 2
Outputs:
- result_field: float32 [2, 2, 4096], P('rhs', None, 'blk')
Inputs may be any that keep to these rules, and one draw needn't show every extreme that they name: `need_owner`: among the 256 entries of one block of targets, at most 64 name the same owner.
All inputs are finite; a program needn't handle non-finite values.
Results may differ from a plain program's by a relative error of at most 0.0003.
Values sent between devices are 32-bit elements; how exact they have to be, the bound alone decides.
No kernel may reach another device: no remote copies, remote signals or barrier semaphores. Data moves between devices by JAX's collectives and lax.ppermute only.
A program may use at most 128 MiB of HBM per device.

v0:
```python
import math

import jax
import jax.numpy as jnp
from jax import lax
from jax.sharding import PartitionSpec as P

WAVE = 8.0
COUPLE = 1.0
SOFT = 0.1
TILE = 512


def unit_normals(angles):
    azimuth = angles[0]
    elevation = angles[1]
    return jnp.stack(
        [
            jnp.cos(azimuth) * jnp.cos(elevation),
            jnp.sin(azimuth) * jnp.cos(elevation),
            jnp.sin(elevation),
        ],
        0,
    )


def kernel_tile(targets, geometry):
    offset_vec = targets[:, :, None] - geometry[0:3, None, :]
    distance = jnp.sqrt(jnp.sum(offset_vec * offset_vec, 0) + SOFT * SOFT)
    facing = jnp.sum(offset_vec * geometry[3:6, None, :], 0)
    single = 1.0 / (4.0 * math.pi * distance)
    double = facing * single / (distance * distance)
    phases = WAVE * distance
    cosine = jnp.cos(phases)
    sines = jnp.sin(phases)
    weight = geometry[6][None, :]
    real_part = weight * (double * (cosine + phases * sines) + COUPLE * single * sines)
    imag_part = weight * (double * (sines - phases * cosine) - COUPLE * single * cosine)
    return (real_part, imag_part)


def apply_tile(targets, geometry, sources):
    real_part, imag_part = kernel_tile(targets, geometry)
    highest = lax.Precision.HIGHEST
    src_real = sources[:, 0, :]
    src_imag = sources[:, 1, :]
    out_real = jnp.einsum("ts,rs->rt", real_part, src_real, precision=highest) - jnp.einsum(
        "ts,rs->rt", imag_part, src_imag, precision=highest
    )
    out_imag = jnp.einsum("ts,rs->rt", real_part, src_imag, precision=highest) + jnp.einsum(
        "ts,rs->rt", imag_part, src_real, precision=highest
    )
    return (out_real, out_imag)


def far_block(running, targets, geometry, sources):
    more_real, more_imag = apply_tile(targets, geometry, sources)
    return (running[0] + more_real, running[1] + more_imag)


def far_piece(running, targets, geometry, flat_sources):
    count_rows = geometry.shape[1]
    side_count = flat_sources.shape[0] // 2
    sources = flat_sources.reshape(side_count, 2, count_rows)
    tile_width = math.gcd(count_rows, TILE)
    blocks = count_rows // tile_width
    geo_tiles = geometry.reshape(7, blocks, tile_width).transpose(1, 0, 2)
    src_tiles = sources.reshape(side_count, 2, blocks, tile_width).transpose(2, 0, 1, 3)

    def advance(partial_sums, tile_pair):
        return (far_block(partial_sums, targets, tile_pair[0], tile_pair[1]), None)

    running, _ = lax.scan(advance, running, (geo_tiles, src_tiles))
    return running


def near_field(needed, near_rows, near_terms):
    looked = needed[:, :, near_rows]
    coef_real = near_terms[0]
    coef_imag = near_terms[1]
    near_real = jnp.sum(coef_real * looked[:, 0] - coef_imag * looked[:, 1], 1)
    near_imag = jnp.sum(coef_real * looked[:, 1] + coef_imag * looked[:, 0], 1)
    return (near_real, near_imag)


def on_device(
    positions, normal_angles, areas, densities, need_owner, need_slot, near_index, near_coef
):
    own_rows = positions.shape[1]
    blk_count = lax.axis_size("blk")
    panels_all = own_rows * blk_count
    normals = unit_normals(normal_angles)
    weights = areas * (1.0 / math.sqrt(panels_all))
    geometry = jnp.concatenate([positions, normals, weights[None, :]], 0)
    owners = need_owner[:, 0]
    need_count = need_slot.shape[0]
    send_density = densities.reshape(2 * densities.shape[0], own_rows)
    side_count = send_density.shape[0] // 2
    target_count = positions.shape[1]
    empty_sum = jnp.zeros((side_count, target_count), jnp.float32)
    far_real, far_imag = far_piece(
        (empty_sum, empty_sum),
        positions,
        lax.all_gather(geometry, "blk", axis=1, tiled=True),
        lax.all_gather(send_density, "blk", axis=1, tiled=True),
    )
    near_sides = densities.shape[0]
    capacity = 4 * need_count // blk_count
    owner_ids = jnp.arange(blk_count, dtype=jnp.int32)
    onehot = (owners[:, None] == owner_ids[None, :]).astype(jnp.int32)
    before = jnp.cumsum(onehot, 0) - onehot
    ranks_in = jnp.sum(before * onehot, 1)
    placed = owners * capacity + ranks_in
    requests = (
        jnp.zeros((blk_count * capacity,), jnp.int32)
        .at[placed]
        .set(need_slot)
        .reshape(blk_count, capacity)
    )
    values = densities[
        :, :, lax.all_to_all(requests, "blk", split_axis=0, concat_axis=0, tiled=True)
    ]
    answers = lax.all_to_all(values, "blk", split_axis=2, concat_axis=2, tiled=True)
    needed = answers.reshape(near_sides, 2, blk_count * capacity)[:, :, placed]
    near_real, near_imag = near_field(needed, near_index, near_coef)
    far_real = far_real + near_real
    far_imag = far_imag + near_imag
    field_real = 0.5 * densities[:, 0] + far_real
    field_imag = 0.5 * densities[:, 1] + far_imag
    result_field = jnp.stack([field_real, field_imag], 1)
    return result_field


def solution(mesh):
    in_specs = (
        P(None, "blk"),
        P(None, "blk"),
        P("blk"),
        P("rhs", None, "blk"),
        P("blk", None),
        P("blk"),
        P(None, "blk"),
        P(None, None, "blk"),
    )
    out_specs = P("rhs", None, "blk")
    return jax.shard_map(
        on_device, mesh=mesh, in_specs=in_specs, out_specs=out_specs, check_vma=False
    )
```

profile of v0, /device:TPU:0, one launch (start us, length us, event | category | flops | bytes accessed | tf_op | source)
XLA Modules:
  0.0 148.3 jit_solution(8561147780038891149)
XLA Ops:
  2.9 1.6 %scatter_custom_fusion = s32[1024]{0:T(1024)S(1)} fusion(s32[256]{0:T(256)S(1)} %bitcast.164, s32[256]{0:T(256)} %param.15, s32[]{:T(128)} %constant.6.clone.1), kind=kCustom, calls=%fused_computation.50 | custom fusion | bytes 4608 | tf_op jit(solution)/shard_map/scatter | solution.py:117
  5.2 7.4 %all-to-all-start = ((s32[16,1,64]{2,1,0:T(1,128)}), s32[16,1,64]{2,1,0:T(1,128)S(1)}, u32[]{:S(2)}, u32[]{:S(2)}) async-start(s32[16,1,64]{2,1,0:T(1,128)} %all_to_all.11), calls=%async_computation | async-start | bytes 16384 | tf_op jit(solution)/shard_map/all_to_all | solution.py:121
  15.6 22.1 %all_gather.7 = f32[7,4096]{1,0:T(8,128)S(1)} all-gather(f32[7,256]{1,0:T(8,128)S(1)} %concatenate.3), channel_id=1, replica_groups=mesh['blk'=16,'rhs'=2] {'blk'}, dimensions={1}, use_global_device_ids=true | all-gather | bytes 121856 | tf_op jit(solution)/shard_map/all_gather | solution.py:104
  37.7 17.7 %all-gather = f32[1,2,4096]{2,1,0:T(2,128)S(1)} all-gather(f32[1,2,256]{2,1,0:T(2,128)} %param.13), channel_id=2, replica_groups=mesh['blk'=16,'rhs'=2] {'blk'}, dimensions={2}, use_global_device_ids=true | all-gather | bytes 34816 | tf_op jit(solution)/shard_map/all_gather | solution.py:105
  55.4 45.6 %while.13 = (s32[]{:T(128)}, f32[1,256]{1,0:T(1,128)S(1)}, f32[1,256]{1,0:T(1,128)S(1)}, f32[8,1,2,512]{3,2,1,0:T(2,128)S(1)}, f32[8,7,512]{2,1,0:T(8,128)S(1)},...) while((s32[]{:T(128)}, f32[1,256]{1,0:T(1,128)S(1)}, f32[1,256]{1,0:T(1,128)S(1)}, ...), condition=%wide.region_3.4_spmd.clone, body=%wide.region_0.3_spmd.clone.sunk | while | flops 10487301 | bytes 5321883 | solution.py:73
  55.4 1.1 fusion.35
  56.5 2.4 %subtract_multiply_fusion.4 = (f32[256,512]{1,0:T(8,128)S(1)}, f32[256,512]{1,0:T(8,128)S(1)}) fusion(f32[256,512]{1,0:T(8,128)S(1)} %get-tuple-element.135, f32[256,512]{1,0:T(8,128)S(1)} %get-tuple-element.136, f32[512]{0:T(512)S(1)} %bitcast.149), kind=kLoop, calls=%fused_computation.8.clone.1 | loop fusion | flops 2490368 | bytes 2099200 | tf_op jit(solution)/shard_map/while/body/eval_jaxpr/mul | solution.py:38
  62.2 2.4 %subtract_multiply_fusion.4 = (f32[256,512]{1,0:T(8,128)S(1)}, f32[256,512]{1,0:T(8,128)S(1)}) fusion(f32[256,512]{1,0:T(8,128)S(1)} %get-tuple-element.135, f32[256,512]{1,0:T(8,128)S(1)} %get-tuple-element.136, f32[512]{0:T(512)S(1)} %bitcast.149), kind=kLoop, calls=%fused_computation.8.clone.1 | loop fusion | flops 2490368 | bytes 2099200 | tf_op jit(solution)/shard_map/while/body/eval_jaxpr/mul | solution.py:38
  67.9 2.4 %subtract_multiply_fusion.4 = (f32[256,512]{1,0:T(8,128)S(1)}, f32[256,512]{1,0:T(8,128)S(1)}) fusion(f32[256,512]{1,0:T(8,128)S(1)} %get-tuple-element.135, f32[256,512]{1,0:T(8,128)S(1)} %get-tuple-element.136, f32[512]{0:T(512)S(1)} %bitcast.149), kind=kLoop, calls=%fused_computation.8.clone.1 | loop fusion | flops 2490368 | bytes 2099200 | tf_op jit(solution)/shard_map/while/body/eval_jaxpr/mul | solution.py:38
  72.5 1.1 fusion.35
  73.6 2.4 %subtract_multiply_fusion.4 = (f32[256,512]{1,0:T(8,128)S(1)}, f32[256,512]{1,0:T(8,128)S(1)}) fusion(f32[256,512]{1,0:T(8,128)S(1)} %get-tuple-element.135, f32[256,512]{1,0:T(8,128)S(1)} %get-tuple-element.136, f32[512]{0:T(512)S(1)} %bitcast.149), kind=kLoop, calls=%fused_computation.8.clone.1 | loop fusion | flops 2490368 | bytes 2099200 | tf_op jit(solution)/shard_map/while/body/eval_jaxpr/mul | solution.py:38
  78.2 1.1 fusion.35
  79.3 2.4 %subtract_multiply_fusion.4 = (f32[256,512]{1,0:T(8,128)S(1)}, f32[256,512]{1,0:T(8,128)S(1)}) fusion(f32[256,512]{1,0:T(8,128)S(1)} %get-tuple-element.135, f32[256,512]{1,0:T(8,128)S(1)} %get-tuple-element.136, f32[512]{0:T(512)S(1)} %bitcast.149), kind=kLoop, calls=%fused_computation.8.clone.1 | loop fusion | flops 2490368 | bytes 2099200 | tf_op jit(solution)/shard_map/while/body/eval_jaxpr/mul | solution.py:38
  83.9 1.1 fusion.35
  85.0 2.4 %subtract_multiply_fusion.4 = (f32[256,512]{1,0:T(8,128)S(1)}, f32[256,512]{1,0:T(8,128)S(1)}) fusion(f32[256,512]{1,0:T(8,128)S(1)} %get-tuple-element.135, f32[256,512]{1,0:T(8,128)S(1)} %get-tuple-element.136, f32[512]{0:T(512)S(1)} %bitcast.149), kind=kLoop, calls=%fused_computation.8.clone.1 | loop fusion | flops 2490368 | bytes 2099200 | tf_op jit(solution)/shard_map/while/body/eval_jaxpr/mul | solution.py:38
  89.6 1.1 fusion.35
  90.7 2.4 %subtract_multiply_fusion.4 = (f32[256,512]{1,0:T(8,128)S(1)}, f32[256,512]{1,0:T(8,128)S(1)}) fusion(f32[256,512]{1,0:T(8,128)S(1)} %get-tuple-element.135, f32[256,512]{1,0:T(8,128)S(1)} %get-tuple-element.136, f32[512]{0:T(512)S(1)} %bitcast.149), kind=kLoop, calls=%fused_computation.8.clone.1 | loop fusion | flops 2490368 | bytes 2099200 | tf_op jit(solution)/shard_map/while/body/eval_jaxpr/mul | solution.py:38
  95.3 1.1 fusion.35
  96.4 2.4 %subtract_multiply_fusion.4 = (f32[256,512]{1,0:T(8,128)S(1)}, f32[256,512]{1,0:T(8,128)S(1)}) fusion(f32[256,512]{1,0:T(8,128)S(1)} %get-tuple-element.135, f32[256,512]{1,0:T(8,128)S(1)} %get-tuple-element.136, f32[512]{0:T(512)S(1)} %bitcast.149), kind=kLoop, calls=%fused_computation.8.clone.1 | loop fusion | flops 2490368 | bytes 2099200 | tf_op jit(solution)/shard_map/while/body/eval_jaxpr/mul | solution.py:38
  101.2 2.8 %gather_fusion = f32[1024,2]{1,0:T(8,128)S(1)} fusion(f32[2,256]{0,1:T(8,128)S(1)} %bitcast.146, s32[1024]{0:T(1024)S(1)} %broadcast_clamp_fusion.1), kind=kCustom, calls=%fused_computation | custom fusion | bytes 20480 | tf_op jit(solution)/shard_map/gather | solution.py:120
  105.0 3.5 %all-to-all-start.1 = ((f32[16,1,128]{2,1,0:T(1,128)}), f32[16,1,128]{2,1,0:T(1,128)S(1)}, u32[]{:S(2)}, u32[]{:S(2)}) async-start(f32[16,1,128]{2,1,0:T(1,128)} %reshape.177), calls=%async_computation.1 | async-start | bytes 16384 | tf_op jit(solution)/shard_map/all_to_all | solution.py:123
  108.5 6.4 %all-to-all-done.1 = f32[16,1,128]{2,1,0:T(1,128)S(1)} async-done(((f32[16,1,128]{2,1,0:T(1,128)}), f32[16,1,128]{2,1,0:T(1,128)S(1)}, u32[]{:S(2)}, u32[]{:S(2)}) %all-to-all-start.1) | async-done | bytes 8224 | tf_op jit(solution)/shard_map/all_to_all | solution.py:123
  117.1 27.7 %gather_fusion.2 = f32[8192,2]{1,0:T(8,128)} fusion(f32[2,256]{0,1:T(8,128)S(1)} %bitcast.143, s32[8192]{0:T(1024)S(1)} %broadcast_clamp_fusion), kind=kCustom, calls=%fused_computation.2 | custom fusion | bytes 163840 | tf_op jit(solution)/shard_map/gather | solution.py:78
  144.8 2.9 %copy.23 = f32[32,256,2]{1,0,2:T(8,128)S(1)} copy(f32[32,256,2]{2,1,0:T(8,128)} %bitcast.142) | data formatting | bytes 131072 | tf_op jit(solution)/shard_map/gather | solution.py:78
  (119 shorter events, 30.1 us)
Async XLA Ops:
  5.2 96.0 %all-to-all-start = ((s32[16,1,64]{2,1,0:T(1,128)}), s32[16,1,64]{2,1,0:T(1,128)S(1)}, u32[]{:S(2)}, u32[]{:S(2)}) async-start(s32[16,1,64]{2,1,0:T(1,128)} %all_to_all.11), calls=%async_computation | async-start | bytes 16384 | tf_op jit(solution)/shard_map/all_to_all | solution.py:121
  55.4 45.6 %copy-start.1 = (f32[1,2,256]{2,1,0:T(2,128)S(1)}, f32[1,2,256]{2,1,0:T(2,128)}, u32[]{:S(2)}) copy-start(f32[1,2,256]{2,1,0:T(2,128)} %param.13) | copy-start | bytes 6148
  105.0 9.9 %all-to-all-start.1 = ((f32[16,1,128]{2,1,0:T(1,128)}), f32[16,1,128]{2,1,0:T(1,128)S(1)}, u32[]{:S(2)}, u32[]{:S(2)}) async-start(f32[16,1,128]{2,1,0:T(1,128)} %reshape.177), calls=%async_computation.1 | async-start | bytes 16384 | tf_op jit(solution)/shard_map/all_to_all | solution.py:123
  144.8 2.9 %copy-start = (f32[2,32,256]{2,1,0:T(8,128)S(1)}, f32[2,32,256]{2,1,0:T(8,128)}, u32[]{:S(2)}) copy-start(f32[2,32,256]{2,1,0:T(8,128)} %param.17) | copy-start | bytes 196612
where the time goes:
time: 149 us; the launch traced here: 148 us
  blocking collectives  39.8 us (27%)
  local copies, waits for them, and re-layouts  39.5 us (27%)
  other arithmetic  34.5 us (23%)
  matrix products  16.7 us (11%)
  starting transfers between devices  10.9 us (7%)
  waiting for transfers between devices  6.36 us (4%)
    gather x2, local copies, waits for them, and re-layouts, near_field(): looked = needed[:, :, near_rows]  30.6 us
    all_gather x1, blocking collectives, on_device(): lax.all_gather(geometry, 'blk', axis=1, tiled=True)  22.1 us
    mul x8, other arithmetic, kernel_tile(): weight * (double * (sines - phases * cosine) - COUPLE * single * cosine)  19.1 us
    all_gather x1, blocking collectives, on_device(): lax.all_gather(send_density, 'blk', axis=1, tiled=True)  17.7 us
    reduce_sum x8, other arithmetic, kernel_tile(): facing = jnp.sum(offset_vec * geometry[3:6, None, :], 0)  8.81 us
    all_to_all x1, starting transfers between devices, on_device(): lax.all_to_all(requests, 'blk', split_axis=0, concat_axis=0, tiled=True)  7.39 us
    all_to_all x1, waiting for transfers between devices, on_device(): lax.all_to_all(values, 'blk', split_axis=2, concat_axis=2, tiled=True)  6.36 us
    dot_general x8, matrix products, apply_tile(): jnp.einsum('ts,rs->rt', imag_part, src_imag, precision=highest)  4.21 us
  transfers between devices with their start and end apart: 2, of which 1 were waited for; matrix products, arithmetic and copies ran while one was open for 33% of the time, Pallas kernels for 0%

commit v1 on v0

v1 whole, which is shorter than its diff:
```python
import functools
import math

import jax
import jax.numpy as jnp
from jax import lax
from jax.experimental import pallas as pl
from jax.experimental.pallas import tpu as pltpu
from jax.sharding import PartitionSpec as P

WAVE = 8.0
SOFT2 = 0.01
LANES = 128
ROWS = 8
KAPPA = WAVE / (2.0 * math.pi)

SIN7 = (4.442867755889893, -7.307443618774414, 3.594788074493408, -0.7843740582466125)
COS6 = (1.4142041206359863, -6.97764253616333, 5.715240955352783, -1.7283549308776855)
SIN11 = (
    4.442883014678955,
    -7.308249473571777,
    3.6064748764038086,
    -0.8474637866020203,
    0.1160099749663353,
    -0.009900202974677086,
)
COS10 = (
    1.4142135381698608,
    -6.9788641929626465,
    5.73988151550293,
    -1.8882750272750854,
    0.3322519063949585,
    -0.03450220078229904,
)
ATAN = (
    0.15915492177009583,
    -0.05305047705769539,
    0.031808558851480484,
    -0.02253829687833786,
    0.016709592193365097,
    -0.011514633893966675,
    0.006331379525363445,
    -0.002292047953233123,
    0.00039099997957237065,
)


def horner(z, coefs):
    acc = coefs[-1]
    for c in coefs[-2::-1]:
        acc = acc * z + c
    return acc


def sincos_turns(turns, sin_coefs, cos_coefs):
    e = turns - jnp.round(turns)
    z = e * e
    s = e * horner(z, sin_coefs)
    c = horner(z, cos_coefs)
    return s * c, 1.0 - s * s


def polar_turns(re, im):
    ax = jnp.abs(re)
    ay = jnp.abs(im)
    big = jnp.maximum(ax, ay)
    ratio = jnp.minimum(ax, ay) / jnp.where(big > 0.0, big, 1.0)
    z = ratio * ratio
    angle = ratio * horner(z, ATAN)
    angle = jnp.where(ay > ax, 0.25 - angle, angle)
    angle = jnp.where(re < 0.0, 0.5 - angle, angle)
    angle = jnp.where(im < 0.0, -angle, angle)
    return big * jnp.sqrt(1.0 + z), angle


def split3(x):
    x1 = x.astype(jnp.bfloat16).astype(jnp.float32)
    rest = x - x1
    x2 = rest.astype(jnp.bfloat16).astype(jnp.float32)
    return x1, x2, rest - x2


FEATURES = 24


def pack_body(pos_ref, ang_ref, area_ref, den_ref, out_ref):
    for h in range(pos_ref.shape[1] // LANES):
        lanes = slice(h * LANES, (h + 1) * LANES)
        base = h * ROWS
        out_ref[base : base + 3, :] = pos_ref[:, lanes]
        out_ref[base + 3 : base + 5, :] = ang_ref[:, lanes]
        out_ref[base + 5 : base + 6, :] = area_ref[:, lanes]
        out_ref[base + 6 : base + 8, :] = den_ref[:, lanes]


def field_body(
    panels_all, blocks, g_ref, owner_ref, slot_ref, index_ref, coef_ref, out_ref, feat, tgt, polar, acc
):
    width = slot_ref.shape[1]
    halves = width // LANES
    me = lax.axis_index("blk")

    def row(k):
        parts = [g_ref[pl.ds(h * ROWS + k, blocks, stride=halves * ROWS), :] for h in range(halves)]
        return jnp.concatenate(parts, 1)

    x = [row(0), row(1), row(2)]
    sa, ca = sincos_turns(row(3) * (0.5 / math.pi), SIN11, COS10)
    se, ce = sincos_turns(row(4) * (0.5 / math.pi), SIN11, COS10)
    weight = row(5) * (KAPPA / (4.0 * math.pi * math.sqrt(panels_all)))
    modulus, angle = polar_turns(row(6), row(7))
    modulus = modulus * weight
    polar[0:blocks, :] = modulus
    polar[blocks : 2 * blocks, :] = angle
    scaled = modulus * (WAVE * KAPPA)
    normal = [ca * ce * scaled, sa * ce * scaled, se * scaled]
    shift = -(x[0] * normal[0] + x[1] * normal[1] + x[2] * normal[2])
    norm2 = (x[0] * x[0] + x[1] * x[1] + x[2] * x[2]) * (KAPPA * KAPPA)

    def put(k, value):
        for h in range(halves):
            feat[pl.ds(h * 2 * FEATURES + k, blocks, stride=halves * 2 * FEATURES), :] = value[
                :, h * LANES : (h + 1) * LANES
            ]

    for c in range(3):
        y1, y2, y3 = split3(x[c] * (-2.0 * KAPPA * KAPPA))
        m1, m2, m3 = split3(normal[c])
        for base, (v1, v2, v3) in ((0, (y1, y2, y3)), (FEATURES, (m1, m2, m3))):
            put(base + c, v1)
            put(base + 3 + c, v2)
            put(base + 6 + c, v3)
            put(base + 9 + c, v1)
            put(base + 12 + c, v2)
            put(base + 15 + c, v1)
    one = jnp.ones_like(weight)
    zero = jnp.zeros_like(weight)
    n1, n2, n3 = split3(norm2 + SOFT2 * KAPPA * KAPPA)
    s1, s2, s3 = split3(shift)
    for k, v in enumerate((one, one, one, n1, n2, n3)):
        put(18 + k, v)
    for k, v in enumerate((zero, zero, zero, s1, s2, s3)):
        put(FEATURES + 18 + k, v)

    t = jnp.concatenate([g_ref[h * ROWS : h * ROWS + 3, :] for h in range(halves)], 1)
    t1, t2, t3 = split3(t)
    tt = t * t
    q1, q2, q3 = split3((tt[0:1] + tt[1:2] + tt[2:3]) * (KAPPA * KAPPA))
    ones3 = jnp.ones_like(t)
    stacked = jnp.concatenate([t1, t1, t1, t2, t2, t3, q1, q2, q3, ones3], 0)
    tgt[...] = stacked.T.astype(jnp.bfloat16)

    acc[...] = jnp.zeros_like(acc)

    @pl.loop(0, blocks)
    def _(b):
        base = b * (halves * 2 * FEATURES)
        weights = jnp.concatenate(
            [
                feat[pl.ds(pl.multiple_of(base + h * 2 * FEATURES, 8), 2 * FEATURES), :]
                for h in range(halves)
            ],
            1,
        ).astype(jnp.bfloat16)
        mod_b = polar[pl.ds(b, 1), :]
        ang_b = polar[pl.ds(blocks + b, 1), :]
        lhs = tgt[...]
        dist2 = jnp.dot(lhs, weights[0:FEATURES], preferred_element_type=jnp.float32)
        facing = jnp.dot(lhs, weights[FEATURES:], preferred_element_type=jnp.float32)
        inv = lax.rsqrt(dist2)
        s, c = sincos_turns(dist2 * inv + ang_b, SIN7, COS6)
        double = facing * (inv * inv)
        b_part = double + inv * mod_b
        a_part = double * (inv * (0.5 / math.pi))
        re = c * a_part + s * b_part
        im = s * a_part - c * b_part
        for part, value in ((0, re), (1, im)):
            total = acc[part]
            for k in range(width // LANES):
                total = total + value[:, k * LANES : (k + 1) * LANES]
            acc[part] = total

    position = owner_ref[...] ^ me
    slot = slot_ref[...]
    den = (row(6), row(7))
    need = []
    for h in range(halves):
        lanes = slice(h * LANES, (h + 1) * LANES)
        slot_h = jnp.broadcast_to(slot[:, lanes], (ROWS, LANES))
        pos_h = jnp.broadcast_to(position[:, lanes], (ROWS, LANES))
        sums = [jnp.zeros((ROWS, LANES), jnp.float32)] * 2
        for p in range(0, blocks, ROWS):
            mine = pos_h == lax.broadcasted_iota(jnp.int32, (ROWS, LANES), 0) + p
            for part in range(2):
                for k in range(halves):
                    got = jnp.take_along_axis(
                        den[part][p : p + ROWS, k * LANES : (k + 1) * LANES], slot_h % LANES, axis=1
                    )
                    sums[part] = sums[part] + jnp.where(mine & (slot_h // LANES == k), got, 0.0)
        need.append([jnp.broadcast_to(jnp.sum(v, 0, keepdims=True), (ROWS, LANES)) for v in sums])

    count = index_ref.shape[0]
    for h in range(halves):
        lanes = slice(h * LANES, (h + 1) * LANES)
        near = [jnp.zeros((ROWS, LANES), jnp.float32)] * 2
        for m in range(0, count, ROWS):
            where = index_ref[m : m + ROWS, lanes]
            picked = []
            for part in range(2):
                got = jnp.zeros((ROWS, LANES), jnp.float32)
                for k in range(halves):
                    one_half = jnp.take_along_axis(need[k][part], where % LANES, axis=1)
                    got = jnp.where(where // LANES == k, one_half, got)
                picked.append(got)
            cr = coef_ref[0, m : m + ROWS, lanes]
            ci = coef_ref[1, m : m + ROWS, lanes]
            near[0] = near[0] + (cr * picked[0] - ci * picked[1])
            near[1] = near[1] + (cr * picked[1] + ci * picked[0])
        for part in range(2):
            own = g_ref[h * ROWS + 6 + part : h * ROWS + 7 + part, :]
            far = jnp.sum(acc[part, lanes, :].T, 0, keepdims=True)
            out_ref[0, part : part + 1, lanes] = (
                0.5 * own + far + jnp.sum(near[part], 0, keepdims=True)
            )


def on_device(
    positions, normal_angles, areas, densities, need_owner, need_slot, near_index, near_coef
):
    width = positions.shape[1]
    blocks = lax.axis_size("blk")
    vmem = pl.BlockSpec(memory_space=pltpu.VMEM)
    gathered = pl.pallas_call(
        pack_body,
        out_shape=jax.ShapeDtypeStruct((ROWS * width // LANES, LANES), jnp.float32),
        in_specs=[vmem] * 4,
        out_specs=vmem,
        name="pack",
    )(positions, normal_angles, areas.reshape(1, width), densities.reshape(2, width))
    step = 1
    while step < blocks:
        other = lax.ppermute(gathered, "blk", [(i, i ^ step) for i in range(blocks)])
        gathered = jnp.concatenate([gathered, other], 0)
        step *= 2
    body = functools.partial(field_body, blocks * width, blocks)
    return pl.pallas_call(
        body,
        out_shape=jax.ShapeDtypeStruct(densities.shape, jnp.float32),
        in_specs=[vmem] * 5,
        out_specs=vmem,
        scratch_shapes=[
            pltpu.VMEM((blocks * 2 * FEATURES * width // LANES, LANES), jnp.float32),
            pltpu.VMEM((width, 3 * ROWS), jnp.bfloat16),
            pltpu.VMEM((2 * blocks, width), jnp.float32),
            pltpu.VMEM((2, width, LANES), jnp.float32),
        ],
        compiler_params=pltpu.CompilerParams(vmem_limit_bytes=32 * 1024 * 1024),
        name="field",
    )(gathered, need_owner.reshape(1, width), need_slot.reshape(1, width), near_index, near_coef)


def solution(mesh):
    in_specs = (
        P(None, "blk"),
        P(None, "blk"),
        P("blk"),
        P("rhs", None, "blk"),
        P("blk", None),
        P("blk"),
        P(None, "blk"),
        P(None, None, "blk"),
    )
    out_specs = P("rhs", None, "blk")
    return jax.shard_map(
        on_device, mesh=mesh, in_specs=in_specs, out_specs=out_specs, check_vma=False
    )
```

time: 149 us -> 26.3 us (0.18)
  blocking collectives: 39.8 us -> 0 us
  local copies, waits for them, and re-layouts: 39.5 us -> 1.38 us
  other arithmetic: 34.5 us -> 0.01 us
  matrix products: 16.7 us -> 0 us
  Pallas kernels: 0 us -> 10.1 us
  starting transfers between devices: 10.9 us -> 8.43 us
    all_gather x2 -> x0, blocking collectives: 39.8 us -> none  [the longest x1 22.1 us: on_device(): lax.all_gather(geometry, 'blk', axis=1, tiled=True)]
    gather x5 -> x0, local copies, waits for them, and re-layouts: 34.3 us -> none  [the longest x2 30.6 us: near_field(): looked = needed[:, :, near_rows]]
    mul x9 -> x0, other arithmetic: 19.7 us -> none  [the longest x8 19.1 us: kernel_tile(): weight * (double * (sines - phases * cosine) - COUPLE * single * cosine)]
    dot_general x32 -> x0, matrix products: 16.7 us -> none  [the longest x8 4.21 us: apply_tile(): jnp.einsum('ts,rs->rt', imag_part, src_imag, precision=highest)]
    all_to_all x2 -> x0, starting transfers between devices: 10.9 us -> none  [the longest x1 7.39 us: on_device(): lax.all_to_all(requests, 'blk', split_axis=0, concat_axis=0, tiled=True)]
    pallas_call x0 -> x2, Pallas kernels: none -> 10.1 us  [the longest x1 8.73 us: on_device(): pl.pallas_call(body, out_shape=jax.ShapeDtypeStruct(densities.shape, jnp....]
    reduce_sum x10 -> x0, other arithmetic: 9.62 us -> none  [the longest x8 8.81 us: kernel_tile(): facing = jnp.sum(offset_vec * geometry[3:6, None, :], 0)]
    ppermute x0 -> x4, starting transfers between devices: none -> 8.43 us  [on_device(): lax.ppermute(gathered, 'blk', [(i, i ^ step) for i in range(blocks)])]
  transfers between devices with their start and end apart: 2 -> 4, of which waited for: 1 -> 4; matrix products, arithmetic and copies ran while one was open for 33% -> 3% of each run, Pallas kernels for 0% -> 0%
where the time goes in v1:
time: 26.3 us; the launch traced here: 26.1 us
  Pallas kernels  10.1 us (38%)
  starting transfers between devices  8.43 us (32%)
  waiting for transfers between devices  6.18 us (23%)
  local copies, waits for them, and re-layouts  1.38 us (5%)
    pallas_call x1, Pallas kernels, on_device(): pl.pallas_call(body, out_shape=jax.ShapeDtypeStruct(densities.shape, jnp....  8.73 us
    ppermute x4, starting transfers between devices, on_device(): lax.ppermute(gathered, 'blk', [(i, i ^ step) for i in range(blocks)])  8.43 us
    ppermute x4, waiting for transfers between devices, on_device(): lax.ppermute(gathered, 'blk', [(i, i ^ step) for i in range(blocks)])  6.18 us
    unnamed x14, local copies, waits for them, and re-layouts  1.37 us
    pallas_call x1, Pallas kernels, on_device(): pl.pallas_call(pack_body, out_shape=jax.ShapeDtypeStruct((ROWS * width //...  1.33 us
  transfers between devices with their start and end apart: 4, of which 4 were waited for; matrix products, arithmetic and copies ran while one was open for 3% of the time, Pallas kernels for 0%

profile of v1, /device:TPU:0, one launch (start us, length us, event | category | flops | bytes accessed | tf_op | source)
XLA Modules:
  0.0 26.1 jit_solution(4651748170602850731)
XLA Ops:
  0.0 1.3 %pack.1 = f32[16,128]{1,0:T(8,128)} custom-call(f32[3,256]{1,0:T(4,128)} %pos_ref.1, f32[2,256]{1,0:T(2,128)} %ang_ref.1, f32[1,256]{1,0:T(1,128)} %bitcast.7, f32[2,256]{1,0:T(2,128)} %bitcast.6), custom_call_target="tpu_custom_call" | custom-call | tf_op jit(solution)/shard_map/pack/pallas_call | solution.py:233
  1.3 0.0 copy-start.4
  1.3 0.5 %collective-permute-start = (f32[16,128]{1,0:T(8,128)}, f32[16,128]{1,0:T(8,128)S(1)}, u32[]{:S(2)}, u32[]{:S(2)}) collective-permute-start(f32[16,128]{1,0:T(8,128)} %pack.1), channel_id=1, source_target_pairs={{0,2},{2,0},{4,6},{6,4},{8,10},{10,8},{12,14},{14,12},{16,18},{18,... | collective-permute-start | bytes 24584 | tf_op jit(solution)/shard_map/ppermute | solution.py:242
  1.8 0.7 %constant_dynamic-update-slice_fusion.4 = f32[256,128]{1,0:T(8,128)S(1)} fusion(f32[16,128]{1,0:T(8,128)} %pack.1), kind=kLoop, calls=%fused_computation.7 | loop fusion | bytes 16384
  2.5 0.3 %collective-permute-done = f32[16,128]{1,0:T(8,128)S(1)} collective-permute-done((f32[16,128]{1,0:T(8,128)}, f32[16,128]{1,0:T(8,128)S(1)}, u32[]{:S(2)}, u32[]{:S(2)}) %collective-permute-start) | collective-permute-done | bytes 8224 | tf_op jit(solution)/shard_map/ppermute | solution.py:242
  2.8 0.0 copy-done.4
  2.8 2.9 %collective-permute-start.1 = (f32[32,128]{1,0:T(8,128)S(1)}, f32[32,128]{1,0:T(8,128)S(1)}, u32[]{:S(2)}, u32[]{:S(2)}) collective-permute-start(f32[32,128]{1,0:T(8,128)S(1)} %pad_maximum_fusion.2), channel_id=1, source_target_pairs={{0,4},{2,6},{4,0},{6,2},{8,12},{10,14},{12,8},{14,10},{16,20},{18,... | collective-permute-start | bytes 49160 | tf_op jit(solution)/shard_map/ppermute | solution.py:242
  5.7 1.7 %collective-permute-done.1 = f32[32,128]{1,0:T(8,128)S(1)} collective-permute-done((f32[32,128]{1,0:T(8,128)S(1)}, f32[32,128]{1,0:T(8,128)S(1)}, u32[]{:S(2)}, u32[]{:S(2)}) %collective-permute-start.1) | collective-permute-done | bytes 16416 | tf_op jit(solution)/shard_map/ppermute | solution.py:242
  7.4 2.1 %collective-permute-start.2 = (f32[64,128]{1,0:T(8,128)S(1)}, f32[64,128]{1,0:T(8,128)S(1)}, u32[]{:S(2)}, u32[]{:S(2)}) collective-permute-start(f32[64,128]{1,0:T(8,128)S(1)} %pad_maximum_fusion.1), channel_id=1, source_target_pairs={{0,8},{2,10},{4,12},{6,14},{8,0},{10,2},{12,4},{14,6},{16,24},{18,... | collective-permute-start | bytes 98312 | tf_op jit(solution)/shard_map/ppermute | solution.py:242
  9.5 1.9 %collective-permute-done.2 = f32[64,128]{1,0:T(8,128)S(1)} collective-permute-done((f32[64,128]{1,0:T(8,128)S(1)}, f32[64,128]{1,0:T(8,128)S(1)}, u32[]{:S(2)}, u32[]{:S(2)}) %collective-permute-start.2) | collective-permute-done | bytes 32800 | tf_op jit(solution)/shard_map/ppermute | solution.py:242
  11.4 3.0 %collective-permute-start.3 = (f32[128,128]{1,0:T(8,128)S(1)}, f32[128,128]{1,0:T(8,128)S(1)}, u32[]{:S(2)}, u32[]{:S(2)}) collective-permute-start(f32[128,128]{1,0:T(8,128)S(1)} %pad_maximum_fusion), channel_id=1, source_target_pairs={{0,16},{2,18},{4,20},{6,22},{8,24},{10,26},{12,28},{14,30},{16,0},... | collective-permute-start | bytes 196616 | tf_op jit(solution)/shard_map/ppermute | solution.py:242
  14.4 0.0 copy-start
  14.4 0.0 copy-start.1
  14.4 2.2 %collective-permute-done.3 = f32[128,128]{1,0:T(8,128)S(1)} collective-permute-done((f32[128,128]{1,0:T(8,128)S(1)}, f32[128,128]{1,0:T(8,128)S(1)}, u32[]{:S(2)}, u32[]{:S(2)}) %collective-permute-start.3) | collective-permute-done | bytes 65568 | tf_op jit(solution)/shard_map/ppermute | solution.py:242
  16.7 0.0 copy-start.3
  16.7 0.0 copy-start.2
  16.7 0.0 copy-done
  16.7 0.0 copy-done.1
  16.7 0.6 %copy-done.3 = s32[256]{0:T(256)S(1)} copy-done((s32[256]{0:T(256)S(1)}, s32[256]{0:T(256)}, u32[]{:S(2)}) %copy-start.3) | copy-done | bytes 1048
  17.3 0.0 copy-done.2
  17.4 8.7 %field.1 = f32[1,2,256]{2,1,0:T(2,128)} custom-call(f32[256,128]{1,0:T(8,128)S(1)} %constant_dynamic-update-slice_fusion.g_ref, s32[1,256]{1,0:T(1,128)S(1)} %bitcast.4, s32[1,256]{1,0:T(1,128)S(1)} %bitcast.5, s32[32,256]{1,0:T(8,128)S(1)} %copy-done.1, f32[2,32,256]{2,1,0:T(8,128)S(1)} %copy-done), custom_call_target="tpu_custom_call" | custom-call | tf_op jit(solution)/shard_map/field/pallas_call | solution.py:246
  (7 shorter events, 0.0 us)
Async XLA Ops:
  1.3 1.5 %copy-start.4 = (f32[16,128]{1,0:T(8,128)S(1)}, f32[16,128]{1,0:T(8,128)}, u32[]{:S(2)}) copy-start(f32[16,128]{1,0:T(8,128)} %pack.1) | copy-start | bytes 24580
  1.3 1.5 %collective-permute-start = (f32[16,128]{1,0:T(8,128)}, f32[16,128]{1,0:T(8,128)S(1)}, u32[]{:S(2)}, u32[]{:S(2)}) collective-permute-start(f32[16,128]{1,0:T(8,128)} %pack.1), channel_id=1, source_target_pairs={{0,2},{2,0},{4,6},{6,4},{8,10},{10,8},{12,14},{14,12},{16,18},{18,... | collective-permute-start | bytes 24584 | tf_op jit(solution)/shard_map/ppermute | solution.py:242
  2.8 4.6 %collective-permute-start.1 = (f32[32,128]{1,0:T(8,128)S(1)}, f32[32,128]{1,0:T(8,128)S(1)}, u32[]{:S(2)}, u32[]{:S(2)}) collective-permute-start(f32[32,128]{1,0:T(8,128)S(1)} %pad_maximum_fusion.2), channel_id=1, source_target_pairs={{0,4},{2,6},{4,0},{6,2},{8,12},{10,14},{12,8},{14,10},{16,20},{18,... | collective-permute-start | bytes 49160 | tf_op jit(solution)/shard_map/ppermute | solution.py:242
  7.4 4.0 %collective-permute-start.2 = (f32[64,128]{1,0:T(8,128)S(1)}, f32[64,128]{1,0:T(8,128)S(1)}, u32[]{:S(2)}, u32[]{:S(2)}) collective-permute-start(f32[64,128]{1,0:T(8,128)S(1)} %pad_maximum_fusion.1), channel_id=1, source_target_pairs={{0,8},{2,10},{4,12},{6,14},{8,0},{10,2},{12,4},{14,6},{16,24},{18,... | collective-permute-start | bytes 98312 | tf_op jit(solution)/shard_map/ppermute | solution.py:242
  11.4 5.3 %collective-permute-start.3 = (f32[128,128]{1,0:T(8,128)S(1)}, f32[128,128]{1,0:T(8,128)S(1)}, u32[]{:S(2)}, u32[]{:S(2)}) collective-permute-start(f32[128,128]{1,0:T(8,128)S(1)} %pad_maximum_fusion), channel_id=1, source_target_pairs={{0,16},{2,18},{4,20},{6,22},{8,24},{10,26},{12,28},{14,30},{16,0},... | collective-permute-start | bytes 196616 | tf_op jit(solution)/shard_map/ppermute | solution.py:242
  14.4 2.3 %copy-start = (f32[2,32,256]{2,1,0:T(8,128)S(1)}, f32[2,32,256]{2,1,0:T(8,128)}, u32[]{:S(2)}) copy-start(f32[2,32,256]{2,1,0:T(8,128)} %coef_ref.1) | copy-start | bytes 196612
  14.4 2.3 %copy-start.1 = (s32[32,256]{1,0:T(8,128)S(1)}, s32[32,256]{1,0:T(8,128)}, u32[]{:S(2)}) copy-start(s32[32,256]{1,0:T(8,128)} %index_ref.1) | copy-start | bytes 98308
  16.7 0.7 %copy-start.3 = (s32[256]{0:T(256)S(1)}, s32[256]{0:T(256)}, u32[]{:S(2)}) copy-start(s32[256]{0:T(256)} %param.13) | copy-start | bytes 3076
  16.7 0.7 %copy-start.2 = (s32[256,1]{0,1:T(1,128)S(1)}, s32[256,1]{0,1:T(1,128)}, u32[]{:S(2)}) copy-start(s32[256,1]{0,1:T(1,128)} %param.12) | copy-start | bytes 3076

commit v2 on v1

--- a/solution.py
+++ b/solution.py
@@ -14,8 +14,6 @@
 ROWS = 8
 KAPPA = WAVE / (2.0 * math.pi)
 
-SIN7 = (4.442867755889893, -7.307443618774414, 3.594788074493408, -0.7843740582466125)
-COS6 = (1.4142041206359863, -6.97764253616333, 5.715240955352783, -1.7283549308776855)
 SIN11 = (
     4.442883014678955,
     -7.308249473571777,
@@ -52,11 +50,11 @@
     return acc
 
 
-def sincos_turns(turns, sin_coefs, cos_coefs):
+def sincos_turns(turns):
     e = turns - jnp.round(turns)
     z = e * e
-    s = e * horner(z, sin_coefs)
-    c = horner(z, cos_coefs)
+    s = e * horner(z, SIN11)
+    c = horner(z, COS10)
     return s * c, 1.0 - s * s
 
 
@@ -81,6 +79,15 @@
 
 
 FEATURES = 24
+CHUNK = 16
+DEPTH = 2
+UNROLL = 8
+SIN5 = (1.5707885026931763, -0.6457120180130005, 0.07766739279031754)
+TOP = 1.0 / SIN5[2]
+SIN_A = SIN5[1] * TOP
+SIN_B = SIN5[0] * TOP
+TOP2 = TOP * TOP
+MU = TOP2 * TOP2 / 8.0
 
 
 def pack_body(pos_ref, ang_ref, area_ref, den_ref, out_ref):
@@ -94,10 +101,11 @@
 
 
 def field_body(
-    panels_all, blocks, g_ref, owner_ref, slot_ref, index_ref, coef_ref, out_ref, feat, tgt, polar, acc
+    panels_all, masks, g_ref, owner_ref, slot_ref, index_ref, coef_ref, out_ref, feat, tgt, polar, acc
 ):
     width = slot_ref.shape[1]
     halves = width // LANES
+    blocks = 1 << len(masks)
     me = lax.axis_index("blk")
 
     def row(k):
@@ -105,9 +113,9 @@
         return jnp.concatenate(parts, 1)
 
     x = [row(0), row(1), row(2)]
-    sa, ca = sincos_turns(row(3) * (0.5 / math.pi), SIN11, COS10)
-    se, ce = sincos_turns(row(4) * (0.5 / math.pi), SIN11, COS10)
-    weight = row(5) * (KAPPA / (4.0 * math.pi * math.sqrt(panels_all)))
+    sa, ca = sincos_turns(row(3) * (0.5 / math.pi))
+    se, ce = sincos_turns(row(4) * (0.5 / math.pi))
+    weight = row(5) * (KAPPA / MU / (4.0 * math.pi * math.sqrt(panels_all)))
     modulus, angle = polar_turns(row(6), row(7))
     modulus = modulus * weight
     polar[0:blocks, :] = modulus
@@ -152,45 +160,75 @@
 
     acc[...] = jnp.zeros_like(acc)
 
-    @pl.loop(0, blocks)
-    def _(b):
+    def load_weights(b):
         base = b * (halves * 2 * FEATURES)
-        weights = jnp.concatenate(
+        return jnp.concatenate(
             [
-                feat[pl.ds(pl.multiple_of(base + h * 2 * FEATURES, 8), 2 * FEATURES), :]
+                feat[pl.ds(pl.multiple_of(base + (h * 2 + j) * FEATURES, 8), FEATURES), :]
+                for j in range(2)
                 for h in range(halves)
             ],
             1,
         ).astype(jnp.bfloat16)
-        mod_b = polar[pl.ds(b, 1), :]
-        ang_b = polar[pl.ds(blocks + b, 1), :]
-        lhs = tgt[...]
-        dist2 = jnp.dot(lhs, weights[0:FEATURES], preferred_element_type=jnp.float32)
-        facing = jnp.dot(lhs, weights[FEATURES:], preferred_element_type=jnp.float32)
+
+    def products(weights, rows):
+        return jnp.dot(tgt[rows, :], weights, preferred_element_type=jnp.float32)
+
+    def add_strip(mod_b, ang_b, res, rows):
+        dist2 = res[:, :width]
+        facing = res[:, width:]
         inv = lax.rsqrt(dist2)
-        s, c = sincos_turns(dist2 * inv + ang_b, SIN7, COS6)
+        turns = dist2 * inv + ang_b
+        e = turns - jnp.round(turns)
+        z = e * e
+        s = ((z + SIN_A) * z + SIN_B) * e
+        q = s * s
+        y = TOP2 - q
+        s = s * (y * lax.rsqrt(y))
+        c = 0.5 * TOP2 - q
+        c, s = MU - s * s, s * c
         double = facing * (inv * inv)
         b_part = double + inv * mod_b
         a_part = double * (inv * (0.5 / math.pi))
         re = c * a_part + s * b_part
         im = s * a_part - c * b_part
         for part, value in ((0, re), (1, im)):
-            total = acc[part]
-            for k in range(width // LANES):
+            total = acc[part, rows, :]
+            for k in range(halves):
                 total = total + value[:, k * LANES : (k + 1) * LANES]
-            acc[part] = total
-
-    position = owner_ref[...] ^ me
+            acc[part, rows, :] = total
+
+    spans = [slice(r, r + CHUNK) for r in range(0, width, CHUNK)]
+    unroll = math.gcd(blocks, UNROLL)
+
+    @pl.loop(0, blocks // unroll)
+    def _(group):
+        for u in range(unroll):
+            b = group * unroll + u
+            weights = load_weights(b)
+            mod_b = polar[pl.ds(b, 1), :]
+            ang_b = polar[pl.ds(blocks + b, 1), :]
+            ready = [products(weights, rows) for rows in spans[:DEPTH]]
+            for k, rows in enumerate(spans):
+                if k + DEPTH < len(spans):
+                    ready.append(products(weights, spans[k + DEPTH]))
+                add_strip(mod_b, ang_b, ready[k], rows)
+
+    owner = owner_ref[...]
     slot = slot_ref[...]
     den = (row(6), row(7))
     need = []
     for h in range(halves):
         lanes = slice(h * LANES, (h + 1) * LANES)
         slot_h = jnp.broadcast_to(slot[:, lanes], (ROWS, LANES))
-        pos_h = jnp.broadcast_to(position[:, lanes], (ROWS, LANES))
+        own_h = jnp.broadcast_to(owner[:, lanes], (ROWS, LANES))
         sums = [jnp.zeros((ROWS, LANES), jnp.float32)] * 2
         for p in range(0, blocks, ROWS):
-            mine = pos_h == lax.broadcasted_iota(jnp.int32, (ROWS, LANES), 0) + p
+            place = lax.broadcasted_iota(jnp.int32, (ROWS, LANES), 0) + p
+            device = me
+            for k, mask in enumerate(masks):
+                device = device ^ (((place >> k) & 1) * mask)
+            mine = own_h == device
             for part in range(2):
                 for k in range(halves):
                     got = jnp.take_along_axis(
@@ -232,17 +270,20 @@
     vmem = pl.BlockSpec(memory_space=pltpu.VMEM)
     gathered = pl.pallas_call(
         pack_body,
-        out_shape=jax.ShapeDtypeStruct((ROWS * width // LANES, LANES), jnp.float32),
+        out_shape=pltpu.VMEM((ROWS * width // LANES, LANES), jnp.float32),
         in_specs=[vmem] * 4,
         out_specs=vmem,
         name="pack",
     )(positions, normal_angles, areas.reshape(1, width), densities.reshape(2, width))
-    step = 1
-    while step < blocks:
-        other = lax.ppermute(gathered, "blk", [(i, i ^ step) for i in range(blocks)])
+    masks = []
+    step = blocks // 2
+    while step:
+        masks.append(step | 1)
+        step //= 2
+    for mask in masks:
+        other = lax.ppermute(gathered, "blk", [(i, i ^ mask) for i in range(blocks)])
         gathered = jnp.concatenate([gathered, other], 0)
-        step *= 2
-    body = functools.partial(field_body, blocks * width, blocks)
+    body = functools.partial(field_body, blocks * width, tuple(masks))
     return pl.pallas_call(
         body,
         out_shape=jax.ShapeDtypeStruct(densities.shape, jnp.float32),

time: 26.3 us -> 21.1 us (0.80)
  Pallas kernels: 10.1 us -> 7.36 us
  starting transfers between devices: 8.43 us -> 7.5 us
  waiting for transfers between devices: 6.18 us -> 5.37 us
  local copies, waits for them, and re-layouts: 1.38 us -> 0.68 us
    pallas_call x1, Pallas kernels: 8.73 us -> 6.63 us  [on_device(): pl.pallas_call(body, out_shape=jax.ShapeDtypeStruct(densities.shape, jnp....]
    ppermute x4, starting transfers between devices: 8.43 us -> 7.5 us  [on_device(): lax.ppermute(gathered, 'blk', [(i, i ^ mask) for i in range(blocks)])]
    ppermute x4, waiting for transfers between devices: 6.18 us -> 5.37 us  [on_device(): lax.ppermute(gathered, 'blk', [(i, i ^ mask) for i in range(blocks)])]
    unnamed x14 -> x12, local copies, waits for them, and re-layouts: 1.37 us -> 0.68 us
    pallas_call x1, Pallas kernels: 1.33 us -> 0.73 us  [on_device(): pl.pallas_call(pack_body, out_shape=pltpu.VMEM((ROWS * width // LANES, LA...]
  transfers between devices with their start and end apart: 4 -> 4, of which waited for: 4 -> 4; matrix products, arithmetic and copies ran while one was open for 3% -> 0% of each run, Pallas kernels for 0% -> 0%
where the time goes in v2:
time: 21.1 us; the launch traced here: 21 us
  starting transfers between devices  7.5 us (36%)
  Pallas kernels  7.36 us (35%)
  waiting for transfers between devices  5.37 us (25%)
  local copies, waits for them, and re-layouts  0.68 us (3%)
    ppermute x4, starting transfers between devices, on_device(): lax.ppermute(gathered, 'blk', [(i, i ^ mask) for i in range(blocks)])  7.5 us
    pallas_call x1, Pallas kernels, on_device(): pl.pallas_call(body, out_shape=jax.ShapeDtypeStruct(densities.shape, jnp....  6.63 us
    ppermute x4, waiting for transfers between devices, on_device(): lax.ppermute(gathered, 'blk', [(i, i ^ mask) for i in range(blocks)])  5.37 us
    pallas_call x1, Pallas kernels, on_device(): pl.pallas_call(pack_body, out_shape=pltpu.VMEM((ROWS * width // LANES, LA...  0.73 us
    unnamed x12, local copies, waits for them, and re-layouts  0.68 us
  transfers between devices with their start and end apart: 4, of which 4 were waited for; matrix products, arithmetic and copies ran while one was open for 0% of the time, Pallas kernels for 0%

profile of v2, /device:TPU:0, one launch (start us, length us, event | category | flops | bytes accessed | tf_op | source)
XLA Modules:
  0.0 21.0 jit_solution(16054319995846910995)
XLA Ops:
  0.0 0.7 %pack.1 = f32[16,128]{1,0:T(8,128)S(1)} custom-call(f32[3,256]{1,0:T(4,128)} %pos_ref.1, f32[2,256]{1,0:T(2,128)} %ang_ref.1, f32[1,256]{1,0:T(1,128)} %bitcast.7, f32[2,256]{1,0:T(2,128)} %bitcast.6), custom_call_target="tpu_custom_call" | custom-call | tf_op jit(solution)/shard_map/pack/pallas_call | solution.py:271
  0.7 3.5 %collective-permute-start = (f32[16,128]{1,0:T(8,128)S(1)}, f32[16,128]{1,0:T(8,128)S(1)}, u32[]{:S(2)}, u32[]{:S(2)}) collective-permute-start(f32[16,128]{1,0:T(8,128)S(1)} %pack.1), channel_id=1, source_target_pairs={{0,18},{2,16},{4,22},{6,20},{8,26},{10,24},{12,30},{14,28},{16,2},... | collective-permute-start | bytes 24584 | tf_op jit(solution)/shard_map/ppermute | solution.py:284
  4.2 1.4 %collective-permute-done = f32[16,128]{1,0:T(8,128)S(1)} collective-permute-done((f32[16,128]{1,0:T(8,128)S(1)}, f32[16,128]{1,0:T(8,128)S(1)}, u32[]{:S(2)}, u32[]{:S(2)}) %collective-permute-start) | collective-permute-done | bytes 8224 | tf_op jit(solution)/shard_map/ppermute | solution.py:284
  5.6 1.9 %collective-permute-start.1 = (f32[32,128]{1,0:T(8,128)S(1)}, f32[32,128]{1,0:T(8,128)S(1)}, u32[]{:S(2)}, u32[]{:S(2)}) collective-permute-start(f32[32,128]{1,0:T(8,128)S(1)} %pad_maximum_fusion.2), channel_id=1, source_target_pairs={{0,10},{2,8},{4,14},{6,12},{8,2},{10,0},{12,6},{14,4},{16,26},{18,... | collective-permute-start | bytes 49160 | tf_op jit(solution)/shard_map/ppermute | solution.py:284
  7.5 1.4 %collective-permute-done.1 = f32[32,128]{1,0:T(8,128)S(1)} collective-permute-done((f32[32,128]{1,0:T(8,128)S(1)}, f32[32,128]{1,0:T(8,128)S(1)}, u32[]{:S(2)}, u32[]{:S(2)}) %collective-permute-start.1) | collective-permute-done | bytes 16416 | tf_op jit(solution)/shard_map/ppermute | solution.py:284
  8.9 1.7 %collective-permute-start.2 = (f32[64,128]{1,0:T(8,128)S(1)}, f32[64,128]{1,0:T(8,128)S(1)}, u32[]{:S(2)}, u32[]{:S(2)}) collective-permute-start(f32[64,128]{1,0:T(8,128)S(1)} %pad_maximum_fusion.1), channel_id=1, source_target_pairs={{0,6},{2,4},{4,2},{6,0},{8,14},{10,12},{12,10},{14,8},{16,22},{18,... | collective-permute-start | bytes 98312 | tf_op jit(solution)/shard_map/ppermute | solution.py:284
  10.6 1.7 %collective-permute-done.2 = f32[64,128]{1,0:T(8,128)S(1)} collective-permute-done((f32[64,128]{1,0:T(8,128)S(1)}, f32[64,128]{1,0:T(8,128)S(1)}, u32[]{:S(2)}, u32[]{:S(2)}) %collective-permute-start.2) | collective-permute-done | bytes 32800 | tf_op jit(solution)/shard_map/ppermute | solution.py:284
  12.3 0.5 %collective-permute-start.3 = (f32[128,128]{1,0:T(8,128)S(1)}, f32[128,128]{1,0:T(8,128)S(1)}, u32[]{:S(2)}, u32[]{:S(2)}) collective-permute-start(f32[128,128]{1,0:T(8,128)S(1)} %pad_maximum_fusion), channel_id=1, source_target_pairs={{0,2},{2,0},{4,6},{6,4},{8,10},{10,8},{12,14},{14,12},{16,18},{18,... | collective-permute-start | bytes 196616 | tf_op jit(solution)/shard_map/ppermute | solution.py:284
  12.7 0.0 copy-start
  12.7 0.0 copy-start.1
  12.7 0.9 %collective-permute-done.3 = f32[128,128]{1,0:T(8,128)S(1)} collective-permute-done((f32[128,128]{1,0:T(8,128)S(1)}, f32[128,128]{1,0:T(8,128)S(1)}, u32[]{:S(2)}, u32[]{:S(2)}) %collective-permute-start.3) | collective-permute-done | bytes 65568 | tf_op jit(solution)/shard_map/ppermute | solution.py:284
  13.6 0.0 copy-start.3
  13.6 0.0 copy-start.2
  13.7 0.0 copy-done
  13.7 0.0 copy-done.1
  13.7 0.6 %copy-done.3 = s32[256]{0:T(256)S(1)} copy-done((s32[256]{0:T(256)S(1)}, s32[256]{0:T(256)}, u32[]{:S(2)}) %copy-start.3) | copy-done | bytes 1048
  14.3 0.0 copy-done.2
  14.3 6.6 %field.1 = f32[1,2,256]{2,1,0:T(2,128)} custom-call(f32[256,128]{1,0:T(8,128)S(1)} %constant_dynamic-update-slice_fusion.g_ref, s32[1,256]{1,0:T(1,128)S(1)} %bitcast.4, s32[1,256]{1,0:T(1,128)S(1)} %bitcast.5, s32[32,256]{1,0:T(8,128)S(1)} %copy-done.1, f32[2,32,256]{2,1,0:T(8,128)S(1)} %copy-done), custom_call_target="tpu_custom_call" | custom-call | tf_op jit(solution)/shard_map/field/pallas_call | solution.py:287
  (8 shorter events, 0.0 us)
Async XLA Ops:
  0.7 4.8 %collective-permute-start = (f32[16,128]{1,0:T(8,128)S(1)}, f32[16,128]{1,0:T(8,128)S(1)}, u32[]{:S(2)}, u32[]{:S(2)}) collective-permute-start(f32[16,128]{1,0:T(8,128)S(1)} %pack.1), channel_id=1, source_target_pairs={{0,18},{2,16},{4,22},{6,20},{8,26},{10,24},{12,30},{14,28},{16,2},... | collective-permute-start | bytes 24584 | tf_op jit(solution)/shard_map/ppermute | solution.py:284
  5.6 3.3 %collective-permute-start.1 = (f32[32,128]{1,0:T(8,128)S(1)}, f32[32,128]{1,0:T(8,128)S(1)}, u32[]{:S(2)}, u32[]{:S(2)}) collective-permute-start(f32[32,128]{1,0:T(8,128)S(1)} %pad_maximum_fusion.2), channel_id=1, source_target_pairs={{0,10},{2,8},{4,14},{6,12},{8,2},{10,0},{12,6},{14,4},{16,26},{18,... | collective-permute-start | bytes 49160 | tf_op jit(solution)/shard_map/ppermute | solution.py:284
  8.9 3.3 %collective-permute-start.2 = (f32[64,128]{1,0:T(8,128)S(1)}, f32[64,128]{1,0:T(8,128)S(1)}, u32[]{:S(2)}, u32[]{:S(2)}) collective-permute-start(f32[64,128]{1,0:T(8,128)S(1)} %pad_maximum_fusion.1), channel_id=1, source_target_pairs={{0,6},{2,4},{4,2},{6,0},{8,14},{10,12},{12,10},{14,8},{16,22},{18,... | collective-permute-start | bytes 98312 | tf_op jit(solution)/shard_map/ppermute | solution.py:284
  12.3 1.4 %collective-permute-start.3 = (f32[128,128]{1,0:T(8,128)S(1)}, f32[128,128]{1,0:T(8,128)S(1)}, u32[]{:S(2)}, u32[]{:S(2)}) collective-permute-start(f32[128,128]{1,0:T(8,128)S(1)} %pad_maximum_fusion), channel_id=1, source_target_pairs={{0,2},{2,0},{4,6},{6,4},{8,10},{10,8},{12,14},{14,12},{16,18},{18,... | collective-permute-start | bytes 196616 | tf_op jit(solution)/shard_map/ppermute | solution.py:284
  12.7 0.9 %copy-start = (f32[2,32,256]{2,1,0:T(8,128)S(1)}, f32[2,32,256]{2,1,0:T(8,128)}, u32[]{:S(2)}) copy-start(f32[2,32,256]{2,1,0:T(8,128)} %coef_ref.1) | copy-start | bytes 196612
  12.7 0.9 %copy-start.1 = (s32[32,256]{1,0:T(8,128)S(1)}, s32[32,256]{1,0:T(8,128)}, u32[]{:S(2)}) copy-start(s32[32,256]{1,0:T(8,128)} %index_ref.1) | copy-start | bytes 98308
  13.6 0.7 %copy-start.3 = (s32[256]{0:T(256)S(1)}, s32[256]{0:T(256)}, u32[]{:S(2)}) copy-start(s32[256]{0:T(256)} %param.13) | copy-start | bytes 3076
  13.6 0.7 %copy-start.2 = (s32[256,1]{0,1:T(1,128)S(1)}, s32[256,1]{0,1:T(1,128)}, u32[]{:S(2)}) copy-start(s32[256,1]{0,1:T(1,128)} %param.12) | copy-start | bytes 3076

commit v3 on v2

--- a/solution.py
+++ b/solution.py
@@ -90,7 +90,9 @@
 MU = TOP2 * TOP2 / 8.0
 
 
-def pack_body(pos_ref, ang_ref, area_ref, den_ref, out_ref):
+def pack_body(pos_ref, ang_ref, area_ref, den_ref, owner_ref, slot_ref, out_ref, need_ref):
+    need_ref[0:1, :] = owner_ref[...]
+    need_ref[1:2, :] = slot_ref[...]
     for h in range(pos_ref.shape[1] // LANES):
         lanes = slice(h * LANES, (h + 1) * LANES)
         base = h * ROWS
@@ -100,17 +102,17 @@
         out_ref[base + 6 : base + 8, :] = den_ref[:, lanes]
 
 
-def field_body(
-    panels_all, masks, g_ref, owner_ref, slot_ref, index_ref, coef_ref, out_ref, feat, tgt, polar, acc
-):
-    width = slot_ref.shape[1]
+def take_row(ref, blocks, halves, k):
+    parts = [ref[pl.ds(h * ROWS + k, blocks, stride=halves * ROWS), :] for h in range(halves)]
+    return jnp.concatenate(parts, 1)
+
+
+def source_features(panels_all, g_ref, feat, polar):
+    blocks, width = polar.shape[0] // 2, polar.shape[1]
     halves = width // LANES
-    blocks = 1 << len(masks)
-    me = lax.axis_index("blk")
 
     def row(k):
-        parts = [g_ref[pl.ds(h * ROWS + k, blocks, stride=halves * ROWS), :] for h in range(halves)]
-        return jnp.concatenate(parts, 1)
+        return take_row(g_ref, blocks, halves, k)
 
     x = [row(0), row(1), row(2)]
     sa, ca = sincos_turns(row(3) * (0.5 / math.pi))
@@ -150,6 +152,9 @@
     for k, v in enumerate((zero, zero, zero, s1, s2, s3)):
         put(FEATURES + 18 + k, v)
 
+
+def target_features(g_ref, tgt):
+    halves = tgt.shape[0] // LANES
     t = jnp.concatenate([g_ref[h * ROWS : h * ROWS + 3, :] for h in range(halves)], 1)
     t1, t2, t3 = split3(t)
     tt = t * t
@@ -158,7 +163,10 @@
     stacked = jnp.concatenate([t1, t1, t1, t2, t2, t3, q1, q2, q3, ones3], 0)
     tgt[...] = stacked.T.astype(jnp.bfloat16)
 
-    acc[...] = jnp.zeros_like(acc)
+
+def add_far(feat, polar, tgt, acc):
+    blocks, width = polar.shape[0] // 2, polar.shape[1]
+    halves = width // LANES
 
     def load_weights(b):
         base = b * (halves * 2 * FEATURES)
@@ -214,9 +222,36 @@
                     ready.append(products(weights, spans[k + DEPTH]))
                 add_strip(mod_b, ang_b, ready[k], rows)
 
-    owner = owner_ref[...]
-    slot = slot_ref[...]
-    den = (row(6), row(7))
+
+def first_body(panels_all, g_ref, acc, tgt, feat, polar):
+    target_features(g_ref, tgt)
+    source_features(panels_all, g_ref, feat, polar)
+    acc[...] = jnp.zeros_like(acc)
+    add_far(feat, polar, tgt, acc)
+
+
+def more_body(panels_all, g_ref, tgt, before, acc, feat, polar):
+    source_features(panels_all, g_ref, feat, polar)
+    add_far(feat, polar, tgt, acc)
+
+
+def last_body(
+    panels_all, masks, g_ref, tgt, before, early_ref, need_ref, index_ref, coef_ref, out_ref, acc, feat, polar
+):
+    width = need_ref.shape[1]
+    halves = width // LANES
+    me = lax.axis_index("blk")
+    source_features(panels_all, g_ref, feat, polar)
+    add_far(feat, polar, tgt, acc)
+
+    owner = need_ref[0:1, :]
+    slot = need_ref[1:2, :]
+    held = polar.shape[0] // 2
+    blocks = 2 * held
+    den = []
+    for k in (6, 7):
+        rows = [take_row(ref, held, halves, k) for ref in (early_ref, g_ref)]
+        den.append(jnp.concatenate(rows, 0))
     need = []
     for h in range(halves):
         lanes = slice(h * LANES, (h + 1) * LANES)
@@ -255,11 +290,24 @@
             near[0] = near[0] + (cr * picked[0] - ci * picked[1])
             near[1] = near[1] + (cr * picked[1] + ci * picked[0])
         for part in range(2):
-            own = g_ref[h * ROWS + 6 + part : h * ROWS + 7 + part, :]
+            own = early_ref[h * ROWS + 6 + part : h * ROWS + 7 + part, :]
             far = jnp.sum(acc[part, lanes, :].T, 0, keepdims=True)
             out_ref[0, part : part + 1, lanes] = (
                 0.5 * own + far + jnp.sum(near[part], 0, keepdims=True)
             )
+
+
+def scratch(blocks, width):
+    return [
+        pltpu.VMEM((blocks * 2 * FEATURES * width // LANES, LANES), jnp.float32),
+        pltpu.VMEM((2 * blocks, width), jnp.float32),
+    ]
+
+
+def far_cost(blocks, width):
+    return pl.CostEstimate(
+        flops=60 * blocks * width * width, bytes_accessed=0, transcendentals=2 * blocks * width * width
+    )
 
 
 def on_device(
@@ -267,37 +315,89 @@
 ):
     width = positions.shape[1]
     blocks = lax.axis_size("blk")
+    panels_all = blocks * width
     vmem = pl.BlockSpec(memory_space=pltpu.VMEM)
-    gathered = pl.pallas_call(
+    params = pltpu.CompilerParams(vmem_limit_bytes=32 * 1024 * 1024)
+    held, need = pl.pallas_call(
         pack_body,
-        out_shape=pltpu.VMEM((ROWS * width // LANES, LANES), jnp.float32),
-        in_specs=[vmem] * 4,
-        out_specs=vmem,
+        out_shape=(
+            pltpu.VMEM((ROWS * width // LANES, LANES), jnp.float32),
+            pltpu.VMEM((2, width), jnp.int32),
+        ),
+        in_specs=[vmem] * 6,
+        out_specs=(vmem, vmem),
         name="pack",
-    )(positions, normal_angles, areas.reshape(1, width), densities.reshape(2, width))
+    )(
+        positions,
+        normal_angles,
+        areas.reshape(1, width),
+        densities.reshape(2, width),
+        need_owner.reshape(1, width),
+        need_slot.reshape(1, width),
+    )
     masks = []
     step = blocks // 2
     while step:
         masks.append(step | 1)
         step //= 2
-    for mask in masks:
-        other = lax.ppermute(gathered, "blk", [(i, i ^ mask) for i in range(blocks)])
-        gathered = jnp.concatenate([gathered, other], 0)
-    body = functools.partial(field_body, blocks * width, tuple(masks))
+
+    def trade(array, mask):
+        return lax.ppermute(array, "blk", [(i, i ^ mask) for i in range(blocks)])
+
+    acc_shape = pltpu.VMEM((2, width, LANES), jnp.float32)
+    tgt_shape = pltpu.VMEM((width, FEATURES), jnp.bfloat16)
+    acc = tgt = None
+    count = 1
+    for k, mask in enumerate(masks):
+        arrived = trade(held, mask)
+        early = held
+        if k == 1:
+            acc, tgt = pl.pallas_call(
+                functools.partial(first_body, panels_all),
+                out_shape=(acc_shape, tgt_shape),
+                in_specs=[vmem],
+                out_specs=(vmem, vmem),
+                scratch_shapes=scratch(count, width),
+                compiler_params=params,
+                cost_estimate=far_cost(count, width),
+                name="far_first",
+            )(held)
+        elif k > 1:
+            acc = pl.pallas_call(
+                functools.partial(more_body, panels_all),
+                out_shape=acc_shape,
+                in_specs=[vmem] * 3,
+                out_specs=vmem,
+                scratch_shapes=scratch(count // 2, width),
+                input_output_aliases={2: 0},
+                compiler_params=params,
+                cost_estimate=far_cost(count // 2, width),
+                name="far_more",
+            )(latest, tgt, acc)
+        if acc is not None:
+            arrived, acc = lax.optimization_barrier((arrived, acc))
+        latest = arrived
+        held = jnp.concatenate([held, arrived], 0)
+        count *= 2
     return pl.pallas_call(
-        body,
-        out_shape=jax.ShapeDtypeStruct(densities.shape, jnp.float32),
-        in_specs=[vmem] * 5,
-        out_specs=vmem,
-        scratch_shapes=[
-            pltpu.VMEM((blocks * 2 * FEATURES * width // LANES, LANES), jnp.float32),
-            pltpu.VMEM((width, 3 * ROWS), jnp.bfloat16),
-            pltpu.VMEM((2 * blocks, width), jnp.float32),
-            pltpu.VMEM((2, width, LANES), jnp.float32),
-        ],
-        compiler_params=pltpu.CompilerParams(vmem_limit_bytes=32 * 1024 * 1024),
+        functools.partial(last_body, panels_all, tuple(masks)),
+        out_shape=(jax.ShapeDtypeStruct(densities.shape, jnp.float32), acc_shape),
+        in_specs=[vmem] * 7,
+        out_specs=(vmem, vmem),
+        scratch_shapes=scratch(count // 2, width),
+        input_output_aliases={2: 1},
+        compiler_params=params,
+        cost_estimate=far_cost(count // 2, width),
         name="field",
-    )(gathered, need_owner.reshape(1, width), need_slot.reshape(1, width), near_index, near_coef)
+    )(
+        latest,
+        tgt,
+        acc,
+        early,
+        need,
+        near_index,
+        near_coef,
+    )[0]
 
 
 def solution(mesh):

time: 21.1 us -> 18 us (0.85)
  waiting for transfers between devices: 5.37 us -> 2.88 us
  local copies, waits for them, and re-layouts: 0.68 us -> 0.02 us
    ppermute x4, waiting for transfers between devices: 5.37 us -> 2.88 us  [trade(): return lax.ppermute(array, 'blk', [(i, i ^ mask) for i in range(blocks)])]
    unnamed x12 -> x6, local copies, waits for them, and re-layouts: 0.68 us -> 0.01 us
    pallas_call x2 -> x5, Pallas kernels: 7.36 us -> 7.26 us  [the longest x1 3.47 us: on_device(): pl.pallas_call(functools.partial(last_body, panels_all, tuple(masks)), ou...]
  transfers between devices with their start and end apart: 4 -> 4, of which waited for: 4 -> 3; matrix products, arithmetic and copies ran while one was open for 0% -> 0% of each run, Pallas kernels for 0% -> 17%
where the time goes in v3:
time: 18 us; the launch traced here: 17.8 us
  starting transfers between devices  7.6 us (42%)
  Pallas kernels  7.26 us (40%)
  waiting for transfers between devices  2.88 us (16%)
    ppermute x4, starting transfers between devices, trade(): return lax.ppermute(array, 'blk', [(i, i ^ mask) for i in range(blocks)])  7.6 us
    pallas_call x1, Pallas kernels, on_device(): pl.pallas_call(functools.partial(last_body, panels_all, tuple(masks)), ou...  3.47 us
    ppermute x4, waiting for transfers between devices, trade(): return lax.ppermute(array, 'blk', [(i, i ^ mask) for i in range(blocks)])  2.88 us
    pallas_call x2, Pallas kernels, on_device(): pl.pallas_call(functools.partial(more_body, panels_all), out_shape=acc_sh...  2.2 us
    pallas_call x1, Pallas kernels, on_device(): pl.pallas_call(functools.partial(first_body, panels_all), out_shape=(acc_...  0.82 us
    pallas_call x1, Pallas kernels, on_device(): pl.pallas_call(pack_body, out_shape=(pltpu.VMEM((ROWS * width // LANES, L...  0.77 us
  transfers between devices with their start and end apart: 4, of which 3 were waited for; matrix products, arithmetic and copies ran while one was open for 0% of the time, Pallas kernels for 17%

profile of v3, /device:TPU:0, one launch (start us, length us, event | category | flops | bytes accessed | tf_op | source)
XLA Modules:
  0.0 17.8 jit_solution(7313940933068477589)
XLA Ops:
  0.0 0.8 %pack.1 = (f32[16,128]{1,0:T(8,128)S(1)}, s32[2,256]{1,0:T(2,128)S(1)}) custom-call(f32[3,256]{1,0:T(4,128)} %pos_ref.1, f32[2,256]{1,0:T(2,128)} %ang_ref.1, f32[1,256]{1,0:T(1,128)} %bitcast.5, f32[2,256]{1,0:T(2,128)} %bitcast.4, s32[1,256]{1,0:T(1,128)} %bitcast.6, s32[1,256]{1,0:T(1,128)} %bitcast.7), custom_call_target="tpu_custom_call" | custom-call | tf_op jit(solution)/shard_map/pack/pallas_call | solution.py:321
  0.8 3.5 %collective-permute-start = (f32[16,128]{1,0:T(8,128)S(1)}, f32[16,128]{1,0:T(8,128)S(1)}, u32[]{:S(2)}, u32[]{:S(2)}) collective-permute-start(f32[16,128]{1,0:T(8,128)S(1)} %get-tuple-element.16), channel_id=1, source_target_pairs={{0,18},{2,16},{4,22},{6,20},{8,26},{10,24},{12,30},{14,28},{16,2},... | collective-permute-start | bytes 24584 | tf_op jit(solution)/shard_map/ppermute | solution.py:345
  4.3 1.4 %collective-permute-done = f32[16,128]{1,0:T(8,128)S(1)} collective-permute-done((f32[16,128]{1,0:T(8,128)S(1)}, f32[16,128]{1,0:T(8,128)S(1)}, u32[]{:S(2)}, u32[]{:S(2)}) %collective-permute-start) | collective-permute-done | bytes 8224 | tf_op jit(solution)/shard_map/ppermute | solution.py:345
  5.6 1.9 %collective-permute-start.1 = (f32[32,128]{1,0:T(8,128)S(1)}, f32[32,128]{1,0:T(8,128)S(1)}, u32[]{:S(2)}, u32[]{:S(2)}) collective-permute-start(f32[32,128]{1,0:T(8,128)S(1)} %get-tuple-element.27.g_ref), channel_id=1, source_target_pairs={{0,10},{2,8},{4,14},{6,12},{8,2},{10,0},{12,6},{14,4},{16,26},{18,... | collective-permute-start | bytes 49160 | tf_op jit(solution)/shard_map/ppermute | solution.py:345
  7.5 0.8 %far_first.1 = (f32[2,256,128]{2,1,0:T(8,128)S(1)}, bf16[256,24]{1,0:T(8,128)(2,1)S(1)}) custom-call(f32[32,128]{1,0:T(8,128)S(1)} %get-tuple-element.27.g_ref), custom_call_target="tpu_custom_call" | custom-call | flops 7864320 | tf_op jit(solution)/shard_map/far_first/pallas_call | solution.py:355
  8.4 0.6 %collective-permute-done.1.g_ref = f32[32,128]{1,0:T(8,128)S(1)} collective-permute-done((f32[32,128]{1,0:T(8,128)S(1)}, f32[32,128]{1,0:T(8,128)S(1)}, u32[]{:S(2)}, u32[]{:S(2)}) %collective-permute-start.1) | collective-permute-done | bytes 16416 | tf_op jit(solution)/shard_map/ppermute | solution.py:345
  9.0 1.7 %collective-permute-start.2 = (f32[64,128]{1,0:T(8,128)S(1)}, f32[64,128]{1,0:T(8,128)S(1)}, u32[]{:S(2)}, u32[]{:S(2)}) collective-permute-start(f32[64,128]{1,0:T(8,128)S(1)} %pad_maximum_fusion), channel_id=1, source_target_pairs={{0,6},{2,4},{4,2},{6,0},{8,14},{10,12},{12,10},{14,8},{16,22},{18,... | collective-permute-start | bytes 98312 | tf_op jit(solution)/shard_map/ppermute | solution.py:345
  10.6 0.8 %far_more.2.before = f32[2,256,128]{2,1,0:T(8,128)S(1)} custom-call(f32[32,128]{1,0:T(8,128)S(1)} %collective-permute-done.1.g_ref, bf16[256,24]{1,0:T(8,128)(2,1)S(1)} %get-tuple-element.19.tgt, f32[2,256,128]{2,1,0:T(8,128)S(1)} %get-tuple-element.20.before), custom_call_target="tpu_custom_call", output_to_operand_aliasing={{}: (2, {})} | custom-call | flops 7864320 | tf_op jit(solution)/shard_map/far_more/pallas_call | solution.py:366
  11.4 0.9 %collective-permute-done.2.g_ref = f32[64,128]{1,0:T(8,128)S(1)} collective-permute-done((f32[64,128]{1,0:T(8,128)S(1)}, f32[64,128]{1,0:T(8,128)S(1)}, u32[]{:S(2)}, u32[]{:S(2)}) %collective-permute-start.2) | collective-permute-done | bytes 32800 | tf_op jit(solution)/shard_map/ppermute | solution.py:345
  12.3 0.0 copy-start
  12.3 0.0 copy-start.1
  12.3 0.6 %collective-permute-start.3 = (f32[128,128]{1,0:T(8,128)S(1)}, f32[128,128]{1,0:T(8,128)S(1)}, u32[]{:S(2)}, u32[]{:S(2)}) collective-permute-start(f32[128,128]{1,0:T(8,128)S(1)} %constant_dynamic-update-slice_fusion.2.early_ref), channel_id=1, source_target_pairs={{0,2},{2,0},{4,6},{6,4},{8,10},{10,8},{12,14},{14,12},{16,18},{18,... | collective-permute-start | bytes 196616 | tf_op jit(solution)/shard_map/ppermute | solution.py:345
  12.9 1.4 %far_more.3.before = f32[2,256,128]{2,1,0:T(8,128)S(1)} custom-call(f32[64,128]{1,0:T(8,128)S(1)} %collective-permute-done.2.g_ref, bf16[256,24]{1,0:T(8,128)(2,1)S(1)} %get-tuple-element.19.tgt, f32[2,256,128]{2,1,0:T(8,128)S(1)} %far_more.2.before), custom_call_target="tpu_custom_call", output_to_operand_aliasing={{}: (2, {})} | custom-call | flops 15728640 | tf_op jit(solution)/shard_map/far_more/pallas_call | solution.py:366
  14.3 0.0 collective-permute-done.3.g_ref
  14.3 0.0 copy-done
  14.3 0.0 copy-done.1
  14.3 3.5 %field.1 = (f32[1,2,256]{2,1,0:T(2,128)}, f32[2,256,128]{2,1,0:T(8,128)S(1)}) custom-call(f32[128,128]{1,0:T(8,128)S(1)} %collective-permute-done.3.g_ref, bf16[256,24]{1,0:T(8,128)(2,1)S(1)} %get-tuple-element.19.tgt, f32[2,256,128]{2,1,0:T(8,128)S(1)} %far_more.3.before, ...), custom_call_target="tpu_custom_call", output_to_operand_aliasing={{1}: (2, {})} | custom-call | flops 31457280 | tf_op jit(solution)/shard_map/field/pallas_call | solution.py:382
  (5 shorter events, 0.0 us)
Async XLA Ops:
  0.8 4.9 %collective-permute-start = (f32[16,128]{1,0:T(8,128)S(1)}, f32[16,128]{1,0:T(8,128)S(1)}, u32[]{:S(2)}, u32[]{:S(2)}) collective-permute-start(f32[16,128]{1,0:T(8,128)S(1)} %get-tuple-element.16), channel_id=1, source_target_pairs={{0,18},{2,16},{4,22},{6,20},{8,26},{10,24},{12,30},{14,28},{16,2},... | collective-permute-start | bytes 24584 | tf_op jit(solution)/shard_map/ppermute | solution.py:345
  5.6 3.3 %collective-permute-start.1 = (f32[32,128]{1,0:T(8,128)S(1)}, f32[32,128]{1,0:T(8,128)S(1)}, u32[]{:S(2)}, u32[]{:S(2)}) collective-permute-start(f32[32,128]{1,0:T(8,128)S(1)} %get-tuple-element.27.g_ref), channel_id=1, source_target_pairs={{0,10},{2,8},{4,14},{6,12},{8,2},{10,0},{12,6},{14,4},{16,26},{18,... | collective-permute-start | bytes 49160 | tf_op jit(solution)/shard_map/ppermute | solution.py:345
  9.0 3.3 %collective-permute-start.2 = (f32[64,128]{1,0:T(8,128)S(1)}, f32[64,128]{1,0:T(8,128)S(1)}, u32[]{:S(2)}, u32[]{:S(2)}) collective-permute-start(f32[64,128]{1,0:T(8,128)S(1)} %pad_maximum_fusion), channel_id=1, source_target_pairs={{0,6},{2,4},{4,2},{6,0},{8,14},{10,12},{12,10},{14,8},{16,22},{18,... | collective-permute-start | bytes 98312 | tf_op jit(solution)/shard_map/ppermute | solution.py:345
  12.3 2.0 %copy-start = (f32[2,32,256]{2,1,0:T(8,128)S(1)}, f32[2,32,256]{2,1,0:T(8,128)}, u32[]{:S(2)}) copy-start(f32[2,32,256]{2,1,0:T(8,128)} %coef_ref.1) | copy-start | bytes 196612
  12.3 2.0 %copy-start.1 = (s32[32,256]{1,0:T(8,128)S(1)}, s32[32,256]{1,0:T(8,128)}, u32[]{:S(2)}) copy-start(s32[32,256]{1,0:T(8,128)} %index_ref.1) | copy-start | bytes 98308
  12.3 2.0 %collective-permute-start.3 = (f32[128,128]{1,0:T(8,128)S(1)}, f32[128,128]{1,0:T(8,128)S(1)}, u32[]{:S(2)}, u32[]{:S(2)}) collective-permute-start(f32[128,128]{1,0:T(8,128)S(1)} %constant_dynamic-update-slice_fusion.2.early_ref), channel_id=1, source_target_pairs={{0,2},{2,0},{4,6},{6,4},{8,10},{10,8},{12,14},{14,12},{16,18},{18,... | collective-permute-start | bytes 196616 | tf_op jit(solution)/shard_map/ppermute | solution.py:345

commit v4 on v3

--- a/solution.py
+++ b/solution.py
@@ -102,17 +102,27 @@
         out_ref[base + 6 : base + 8, :] = den_ref[:, lanes]
 
 
-def take_row(ref, blocks, halves, k):
-    parts = [ref[pl.ds(h * ROWS + k, blocks, stride=halves * ROWS), :] for h in range(halves)]
-    return jnp.concatenate(parts, 1)
-
-
-def source_features(panels_all, g_ref, feat, polar):
+def take_row(parts, halves, k):
+    step = halves * ROWS
+    rows = [
+        jnp.concatenate(
+            [
+                ref[pl.ds(first * step + h * ROWS + k, count, stride=step if count > 1 else None), :]
+                for h in range(halves)
+            ],
+            1,
+        )
+        for ref, first, count in parts
+    ]
+    return jnp.concatenate(rows, 0)
+
+
+def source_features(panels_all, parts, feat, polar):
     blocks, width = polar.shape[0] // 2, polar.shape[1]
     halves = width // LANES
 
     def row(k):
-        return take_row(g_ref, blocks, halves, k)
+        return take_row(parts, halves, k)
 
     x = [row(0), row(1), row(2)]
     sa, ca = sincos_turns(row(3) * (0.5 / math.pi))
@@ -128,8 +138,9 @@
     norm2 = (x[0] * x[0] + x[1] * x[1] + x[2] * x[2]) * (KAPPA * KAPPA)
 
     def put(k, value):
+        stride = halves * 2 * FEATURES if blocks > 1 else None
         for h in range(halves):
-            feat[pl.ds(h * 2 * FEATURES + k, blocks, stride=halves * 2 * FEATURES), :] = value[
+            feat[pl.ds(h * 2 * FEATURES + k, blocks, stride=stride), :] = value[
                 :, h * LANES : (h + 1) * LANES
             ]
 
@@ -153,18 +164,19 @@
         put(FEATURES + 18 + k, v)
 
 
-def target_features(g_ref, tgt):
-    halves = tgt.shape[0] // LANES
+def target_features(g_ref, tgt, first):
+    halves = tgt.shape[0] // 2 // LANES
+    width = halves * LANES
     t = jnp.concatenate([g_ref[h * ROWS : h * ROWS + 3, :] for h in range(halves)], 1)
     t1, t2, t3 = split3(t)
     tt = t * t
     q1, q2, q3 = split3((tt[0:1] + tt[1:2] + tt[2:3]) * (KAPPA * KAPPA))
     ones3 = jnp.ones_like(t)
     stacked = jnp.concatenate([t1, t1, t1, t2, t2, t3, q1, q2, q3, ones3], 0)
-    tgt[...] = stacked.T.astype(jnp.bfloat16)
-
-
-def add_far(feat, polar, tgt, acc):
+    tgt[first : first + width, :] = stacked.T.astype(jnp.bfloat16)
+
+
+def add_far(feat, polar, tgt, acc, first_block, count, top, bottom):
     blocks, width = polar.shape[0] // 2, polar.shape[1]
     halves = width // LANES
 
@@ -206,13 +218,13 @@
                 total = total + value[:, k * LANES : (k + 1) * LANES]
             acc[part, rows, :] = total
 
-    spans = [slice(r, r + CHUNK) for r in range(0, width, CHUNK)]
-    unroll = math.gcd(blocks, UNROLL)
-
-    @pl.loop(0, blocks // unroll)
+    spans = [slice(r, r + CHUNK) for r in range(top, bottom, CHUNK)]
+    unroll = math.gcd(count, UNROLL * width // (bottom - top))
+
+    @pl.loop(0, count // unroll)
     def _(group):
         for u in range(unroll):
-            b = group * unroll + u
+            b = first_block + group * unroll + u
             weights = load_weights(b)
             mod_b = polar[pl.ds(b, 1), :]
             ang_b = polar[pl.ds(blocks + b, 1), :]
@@ -223,35 +235,82 @@
                 add_strip(mod_b, ang_b, ready[k], rows)
 
 
-def first_body(panels_all, g_ref, acc, tgt, feat, polar):
-    target_features(g_ref, tgt)
-    source_features(panels_all, g_ref, feat, polar)
+def far_sums(acc, first, width):
+    return [
+        jnp.concatenate(
+            [
+                jnp.sum(acc[part, h : h + LANES, :].T, 0, keepdims=True)
+                for h in range(first, first + width, LANES)
+            ],
+            1,
+        )
+        for part in range(2)
+    ]
+
+
+def own_body(panels_all, own_ref, index_in, coef_in, acc, tgt, index_out, coef_out, feat, polar, sems):
+    width = polar.shape[1]
+    copies = [
+        pltpu.make_async_copy(index_in, index_out, sems.at[0]),
+        pltpu.make_async_copy(coef_in, coef_out, sems.at[1]),
+    ]
+    for copy in copies:
+        copy.start()
+    target_features(own_ref, tgt, 0)
+    source_features(panels_all, [(own_ref, 0, 1)], feat, polar)
     acc[...] = jnp.zeros_like(acc)
-    add_far(feat, polar, tgt, acc)
-
-
-def more_body(panels_all, g_ref, tgt, before, acc, feat, polar):
-    source_features(panels_all, g_ref, feat, polar)
-    add_far(feat, polar, tgt, acc)
+    add_far(feat, polar, tgt, acc, 0, 1, 0, width)
+    for copy in copies:
+        copy.wait()
+
+
+def mate_body(panels_all, own_ref, mate_ref, g_ref, acc_in, tgt_in, acc, tgt, feat, polar):
+    width = polar.shape[1]
+    target_features(mate_ref, tgt, width)
+    source_features(panels_all, [(own_ref, 0, 1), (g_ref, 0, 1)], feat, polar)
+    add_far(feat, polar, tgt, acc, 0, 1, width, 2 * width)
+    add_far(feat, polar, tgt, acc, 1, 1, 0, 2 * width)
+
+
+def both_body(panels_all, final, g_ref, tgt, acc_in, acc, *rest):
+    feat, polar = rest[-2:]
+    blocks, width = polar.shape[0] // 2, polar.shape[1]
+    source_features(panels_all, [(g_ref, 0, blocks)], feat, polar)
+    add_far(feat, polar, tgt, acc, 0, blocks, 0, 2 * width)
+    if final:
+        gift = rest[0]
+        gift[...] = jnp.zeros_like(gift)
+        sums = far_sums(acc, width, width)
+        for part in range(2):
+            for h in range(width // LANES):
+                k = part * (width // LANES) + h
+                gift[k : k + 1, :] = sums[part][:, h * LANES : (h + 1) * LANES]
+
+
+def self_body(panels_all, g_ref, tgt, acc_in, acc, feat, polar):
+    blocks, width = polar.shape[0] // 2, polar.shape[1]
+    source_features(panels_all, [(g_ref, 0, blocks)], feat, polar)
+    add_far(feat, polar, tgt, acc, 0, blocks, 0, width)
 
 
 def last_body(
-    panels_all, masks, g_ref, tgt, before, early_ref, need_ref, index_ref, coef_ref, out_ref, acc, feat, polar
+    panels_all, masks, g_ref, tgt, acc_in, early_ref, need_ref, index_ref, coef_ref, out_ref, acc, feat, polar
 ):
     width = need_ref.shape[1]
     halves = width // LANES
     me = lax.axis_index("blk")
-    source_features(panels_all, g_ref, feat, polar)
-    add_far(feat, polar, tgt, acc)
+    fresh = polar.shape[0] // 2
+    held = 2 * fresh
+    source_features(panels_all, [(g_ref, fresh, fresh)], feat, polar)
+    add_far(feat, polar, tgt, acc, 0, fresh, 0, width)
+    far = far_sums(acc, 0, width)
 
     owner = need_ref[0:1, :]
     slot = need_ref[1:2, :]
-    held = polar.shape[0] // 2
     blocks = 2 * held
     den = []
     for k in (6, 7):
-        rows = [take_row(ref, held, halves, k) for ref in (early_ref, g_ref)]
-        den.append(jnp.concatenate(rows, 0))
+        den.append(take_row([(early_ref, 0, held), (g_ref, 0, held)], halves, k))
     need = []
     for h in range(halves):
         lanes = slice(h * LANES, (h + 1) * LANES)
@@ -291,9 +350,10 @@
             near[1] = near[1] + (cr * picked[1] + ci * picked[0])
         for part in range(2):
             own = early_ref[h * ROWS + 6 + part : h * ROWS + 7 + part, :]
-            far = jnp.sum(acc[part, lanes, :].T, 0, keepdims=True)
+            k = blocks * halves * ROWS // 2 + part * halves + h
+            gift = g_ref[k : k + 1, :]
             out_ref[0, part : part + 1, lanes] = (
-                0.5 * own + far + jnp.sum(near[part], 0, keepdims=True)
+                0.5 * own + (far[part][:, lanes] + gift) + jnp.sum(near[part], 0, keepdims=True)
             )
 
 
@@ -344,60 +404,91 @@
     def trade(array, mask):
         return lax.ppermute(array, "blk", [(i, i ^ mask) for i in range(blocks)])
 
-    acc_shape = pltpu.VMEM((2, width, LANES), jnp.float32)
-    tgt_shape = pltpu.VMEM((width, FEATURES), jnp.bfloat16)
-    acc = tgt = None
+    def kernel(body, out_shape, operands, work, blocks_in, aliases=None):
+        several = isinstance(out_shape, tuple)
+        return pl.pallas_call(
+            body,
+            out_shape=out_shape,
+            in_specs=[vmem] * len(operands),
+            out_specs=(vmem,) * len(out_shape) if several else vmem,
+            scratch_shapes=scratch(blocks_in, width),
+            input_output_aliases=aliases or {},
+            compiler_params=params,
+            cost_estimate=far_cost(work, width),
+            name="far",
+        )(*operands)
+
+    acc_shape = pltpu.VMEM((2, 2 * width, LANES), jnp.float32)
+    tgt_shape = pltpu.VMEM((2 * width, FEATURES), jnp.bfloat16)
+    gift_shape = pltpu.VMEM((ROWS, LANES), jnp.float32)
+    own = latest = held
+    early = mate = acc = tgt = gift = None
     count = 1
     for k, mask in enumerate(masks):
-        arrived = trade(held, mask)
         early = held
-        if k == 1:
-            acc, tgt = pl.pallas_call(
-                functools.partial(first_body, panels_all),
-                out_shape=(acc_shape, tgt_shape),
-                in_specs=[vmem],
-                out_specs=(vmem, vmem),
-                scratch_shapes=scratch(count, width),
+        send = held if gift is None else jnp.concatenate([held, gift], 0)
+        send, latest = lax.optimization_barrier((send, latest))
+        arrived = trade(send, mask)
+        if k == 0:
+            acc, tgt, index, coef = pl.pallas_call(
+                functools.partial(own_body, panels_all),
+                out_shape=(
+                    acc_shape,
+                    tgt_shape,
+                    pltpu.VMEM(near_index.shape, near_index.dtype),
+                    pltpu.VMEM(near_coef.shape, near_coef.dtype),
+                ),
+                in_specs=[vmem, pl.BlockSpec(memory_space=pltpu.HBM), pl.BlockSpec(memory_space=pltpu.HBM)],
+                out_specs=(vmem,) * 4,
+                scratch_shapes=scratch(1, width) + [pltpu.SemaphoreType.DMA((2,))],
                 compiler_params=params,
-                cost_estimate=far_cost(count, width),
-                name="far_first",
-            )(held)
-        elif k > 1:
-            acc = pl.pallas_call(
-                functools.partial(more_body, panels_all),
-                out_shape=acc_shape,
-                in_specs=[vmem] * 3,
-                out_specs=vmem,
-                scratch_shapes=scratch(count // 2, width),
-                input_output_aliases={2: 0},
-                compiler_params=params,
-                cost_estimate=far_cost(count // 2, width),
-                name="far_more",
-            )(latest, tgt, acc)
-        if acc is not None:
-            arrived, acc = lax.optimization_barrier((arrived, acc))
+                cost_estimate=far_cost(1, width),
+                name="far",
+            )(
+                own,
+                pltpu.with_memory_space_constraint(near_index, pltpu.HBM),
+                pltpu.with_memory_space_constraint(near_coef, pltpu.HBM),
+            )
+            own, acc = lax.optimization_barrier((own, acc))
+            mate = trade(own, 1)
+        elif k == 1:
+            acc, tgt = kernel(
+                functools.partial(mate_body, panels_all),
+                (acc_shape, tgt_shape),
+                (own, mate, latest, acc, tgt),
+                3,
+                2,
+                {3: 0, 4: 1},
+            )
+        elif k < len(masks) - 1:
+            final = k == len(masks) - 2
+            out = kernel(
+                functools.partial(both_body, panels_all, final),
+                (acc_shape, gift_shape) if final else (acc_shape,),
+                (latest, tgt, acc),
+                count,
+                count // 2,
+                {2: 0},
+            )
+            acc = out[0]
+            gift = out[1] if final else None
+        else:
+            acc = kernel(
+                functools.partial(self_body, panels_all), acc_shape, (latest, tgt, acc), count // 2, count // 2, {2: 0}
+            )
+        arrived, acc = lax.optimization_barrier((arrived, acc))
         latest = arrived
         held = jnp.concatenate([held, arrived], 0)
         count *= 2
-    return pl.pallas_call(
+    out = kernel(
         functools.partial(last_body, panels_all, tuple(masks)),
-        out_shape=(jax.ShapeDtypeStruct(densities.shape, jnp.float32), acc_shape),
-        in_specs=[vmem] * 7,
-        out_specs=(vmem, vmem),
-        scratch_shapes=scratch(count // 2, width),
-        input_output_aliases={2: 1},
-        compiler_params=params,
-        cost_estimate=far_cost(count // 2, width),
-        name="field",
-    )(
-        latest,
-        tgt,
-        acc,
-        early,
-        need,
-        near_index,
-        near_coef,
-    )[0]
+        (jax.ShapeDtypeStruct(densities.shape, jnp.float32), acc_shape),
+        (latest, tgt, acc, early, need, index, coef),
+        count // 4,
+        count // 4,
+        {2: 1},
+    )
+    return out[0]
 
 
 def solution(mesh):

time: 18 us -> 16.7 us (0.928)
  waiting for transfers between devices: 2.88 us -> 1.23 us
  Pallas kernels: 7.26 us -> 8.06 us
  starting transfers between devices: 7.6 us -> 7.14 us
    ppermute x4 -> x5, waiting for transfers between devices: 2.88 us -> 1.23 us  [trade(): return lax.ppermute(array, 'blk', [(i, i ^ mask) for i in range(blocks)])]
    pallas_call x4 -> x5, Pallas kernels: 6.49 us -> 7.29 us  [the longest x4 6.23 us: kernel(): pl.pallas_call(body, out_shape=out_shape, in_specs=[vmem] * len(operands)...]
    ppermute x4 -> x5, starting transfers between devices: 7.6 us -> 7.14 us  [trade(): return lax.ppermute(array, 'blk', [(i, i ^ mask) for i in range(blocks)])]
  transfers between devices with their start and end apart: 4 -> 5, of which waited for: 3 -> 2; matrix products, arithmetic and copies ran while one was open for 0% -> 0% of each run, Pallas kernels for 17% -> 31%
where the time goes in v4:
time: 16.7 us; the launch traced here: 16.5 us
  Pallas kernels  8.06 us (48%)
  starting transfers between devices  7.14 us (43%)
  waiting for transfers between devices  1.23 us (7%)
    ppermute x5, starting transfers between devices, trade(): return lax.ppermute(array, 'blk', [(i, i ^ mask) for i in range(blocks)])  7.14 us
    pallas_call x4, Pallas kernels, kernel(): pl.pallas_call(body, out_shape=out_shape, in_specs=[vmem] * len(operands)...  6.23 us
    ppermute x5, waiting for transfers between devices, trade(): return lax.ppermute(array, 'blk', [(i, i ^ mask) for i in range(blocks)])  1.23 us
    pallas_call x1, Pallas kernels, on_device(): pl.pallas_call(functools.partial(own_body, panels_all), out_shape=(acc_sh...  1.06 us
    pallas_call x1, Pallas kernels, on_device(): pl.pallas_call(pack_body, out_shape=(pltpu.VMEM((ROWS * width // LANES, L...  0.77 us
  transfers between devices with their start and end apart: 5, of which 2 were waited for; matrix products, arithmetic and copies ran while one was open for 0% of the time, Pallas kernels for 31%

profile of v4, /device:TPU:0, one launch (start us, length us, event | category | flops | bytes accessed | tf_op | source)
XLA Modules:
  0.0 16.5 jit_solution(14296922782965719309)
XLA Ops:
  0.0 0.8 %pack.1 = (f32[16,128]{1,0:T(8,128)S(1)}, s32[2,256]{1,0:T(2,128)S(1)}) custom-call(f32[3,256]{1,0:T(4,128)} %pos_ref.1, f32[2,256]{1,0:T(2,128)} %ang_ref.1, f32[1,256]{1,0:T(1,128)} %bitcast.5, f32[2,256]{1,0:T(2,128)} %bitcast.4, s32[1,256]{1,0:T(1,128)} %bitcast.6, s32[1,256]{1,0:T(1,128)} %bitcast.7), custom_call_target="tpu_custom_call" | custom-call | tf_op jit(solution)/shard_map/pack/pallas_call | solution.py:381
  0.8 3.5 %collective-permute-start = (f32[16,128]{1,0:T(8,128)S(1)}, f32[16,128]{1,0:T(8,128)S(1)}, u32[]{:S(2)}, u32[]{:S(2)}) collective-permute-start(f32[16,128]{1,0:T(8,128)S(1)} %get-tuple-element.39.own_ref), channel_id=1, source_target_pairs={{0,18},{2,16},{4,22},{6,20},{8,26},{10,24},{12,30},{14,28},{16,2},... | collective-permute-start | bytes 24584 | tf_op jit(solution)/shard_map/ppermute | solution.py:405
  4.3 1.1 %far.5 = (f32[2,512,128]{2,1,0:T(8,128)S(1)}, bf16[512,24]{1,0:T(8,128)(2,1)S(1)}, s32[32,256]{1,0:T(8,128)S(1)}, f32[2,32,256]{2,1,0:T(8,128)S(1)}) custom-call(f32[16,128]{1,0:T(8,128)S(1)} %get-tuple-element.39.own_ref, s32[32,256]{1,0:T(8,128)} %index_in.1, f32[2,32,256]{2,1,0:T(8,128)} %coef_in.1), custom_call_target="tpu_custom_call" | custom-call | flops 3932160 | tf_op jit(solution)/shard_map/far/pallas_call | solution.py:433
  5.3 0.7 %collective-permute-start.2 = (f32[16,128]{1,0:T(8,128)S(1)}, f32[16,128]{1,0:T(8,128)S(1)}, u32[]{:S(2)}, u32[]{:S(2)}) collective-permute-start(f32[16,128]{1,0:T(8,128)S(1)} %get-tuple-element.39.own_ref), channel_id=1, source_target_pairs={{0,2},{2,0},{4,6},{6,4},{8,10},{10,8},{12,14},{14,12},{16,18},{18,... | collective-permute-start | bytes 24584 | tf_op jit(solution)/shard_map/ppermute | solution.py:405
  6.1 0.0 collective-permute-done.g_ref
  6.1 1.4 %collective-permute-start.1 = (f32[32,128]{1,0:T(8,128)S(1)}, f32[32,128]{1,0:T(8,128)S(1)}, u32[]{:S(2)}, u32[]{:S(2)}) collective-permute-start(f32[32,128]{1,0:T(8,128)S(1)} %pad_maximum_fusion.2), channel_id=1, source_target_pairs={{0,10},{2,8},{4,14},{6,12},{8,2},{10,0},{12,6},{14,4},{16,26},{18,... | collective-permute-start | bytes 49160 | tf_op jit(solution)/shard_map/ppermute | solution.py:405
  7.5 0.0 collective-permute-done.2.mate_ref
  7.5 1.1 %far.6 = (f32[2,512,128]{2,1,0:T(8,128)S(1)}, bf16[512,24]{1,0:T(8,128)(2,1)S(1)}) custom-call(f32[16,128]{1,0:T(8,128)S(1)} %get-tuple-element.39.own_ref, f32[16,128]{1,0:T(8,128)S(1)} %collective-permute-done.2.mate_ref, f32[16,128]{1,0:T(8,128)S(1)} %collective-permute-done.g_ref, ...), custom_call_target="tpu_custom_call", output_to_operand_aliasing={{0}: (3, {}), {1}: (4, {})} | custom-call | flops 11796480 | tf_op jit(solution)/shard_map/far/pallas_call | solution.py:409
  8.7 0.6 %collective-permute-done.1.g_ref = f32[32,128]{1,0:T(8,128)S(1)} collective-permute-done((f32[32,128]{1,0:T(8,128)S(1)}, f32[32,128]{1,0:T(8,128)S(1)}, u32[]{:S(2)}, u32[]{:S(2)}) %collective-permute-start.1) | collective-permute-done | bytes 16416 | tf_op jit(solution)/shard_map/ppermute | solution.py:405
  9.3 1.3 %collective-permute-start.3 = (f32[64,128]{1,0:T(8,128)S(1)}, f32[64,128]{1,0:T(8,128)S(1)}, u32[]{:S(2)}, u32[]{:S(2)}) collective-permute-start(f32[64,128]{1,0:T(8,128)S(1)} %pad_maximum_fusion.1), channel_id=1, source_target_pairs={{0,6},{2,4},{4,2},{6,0},{8,14},{10,12},{12,10},{14,8},{16,22},{18,... | collective-permute-start | bytes 98312 | tf_op jit(solution)/shard_map/ppermute | solution.py:405
  10.6 1.5 %far.7 = (f32[2,512,128]{2,1,0:T(8,128)S(1)}, f32[8,128]{1,0:T(8,128)S(1)}) custom-call(f32[32,128]{1,0:T(8,128)S(1)} %collective-permute-done.1.g_ref, bf16[512,24]{1,0:T(8,128)(2,1)S(1)} %get-tuple-element.47.tgt, f32[2,512,128]{2,1,0:T(8,128)S(1)} %get-tuple-element.48.acc_in), custom_call_target="tpu_custom_call", output_to_operand_aliasing={{0}: (2, {})} | custom-call | flops 15728640 | tf_op jit(solution)/shard_map/far/pallas_call | solution.py:409
  12.1 0.6 %collective-permute-done.3.g_ref = f32[64,128]{1,0:T(8,128)S(1)} collective-permute-done((f32[64,128]{1,0:T(8,128)S(1)}, f32[64,128]{1,0:T(8,128)S(1)}, u32[]{:S(2)}, u32[]{:S(2)}) %collective-permute-start.3) | collective-permute-done | bytes 32800 | tf_op jit(solution)/shard_map/ppermute | solution.py:405
  12.7 0.1 collective-permute-start.4
  12.8 1.4 %far.8.acc_in = f32[2,512,128]{2,1,0:T(8,128)S(1)} custom-call(f32[64,128]{1,0:T(8,128)S(1)} %collective-permute-done.3.g_ref, bf16[512,24]{1,0:T(8,128)(2,1)S(1)} %get-tuple-element.47.tgt, f32[2,512,128]{2,1,0:T(8,128)S(1)} %get-tuple-element.54.acc_in), custom_call_target="tpu_custom_call", output_to_operand_aliasing={{}: (2, {})} | custom-call | flops 15728640 | tf_op jit(solution)/shard_map/far/pallas_call | solution.py:409
  14.3 0.0 collective-permute-done.4.g_ref
  14.3 2.2 %far.9 = (f32[1,2,256]{2,1,0:T(2,128)}, f32[2,512,128]{2,1,0:T(8,128)S(1)}) custom-call(f32[136,128]{1,0:T(8,128)S(1)} %collective-permute-done.4.g_ref, bf16[512,24]{1,0:T(8,128)(2,1)S(1)} %get-tuple-element.47.tgt, f32[2,512,128]{2,1,0:T(8,128)S(1)} %far.8.acc_in, f32[128,128]{1,0:T(8,128)S(1)} %pad_maximum_fusion.early_ref, ...), custom_call_target="tpu_custom_call", output_to_operand_aliasing={{1}: (2, {})} | custom-call | flops 15728640 | tf_op jit(solution)/shard_map/far/pallas_call | solution.py:409
  (8 shorter events, 0.0 us)
Async XLA Ops:
  0.8 5.3 %collective-permute-start = (f32[16,128]{1,0:T(8,128)S(1)}, f32[16,128]{1,0:T(8,128)S(1)}, u32[]{:S(2)}, u32[]{:S(2)}) collective-permute-start(f32[16,128]{1,0:T(8,128)S(1)} %get-tuple-element.39.own_ref), channel_id=1, source_target_pairs={{0,18},{2,16},{4,22},{6,20},{8,26},{10,24},{12,30},{14,28},{16,2},... | collective-permute-start | bytes 24584 | tf_op jit(solution)/shard_map/ppermute | solution.py:405
  5.3 2.2 %collective-permute-start.2 = (f32[16,128]{1,0:T(8,128)S(1)}, f32[16,128]{1,0:T(8,128)S(1)}, u32[]{:S(2)}, u32[]{:S(2)}) collective-permute-start(f32[16,128]{1,0:T(8,128)S(1)} %get-tuple-element.39.own_ref), channel_id=1, source_target_pairs={{0,2},{2,0},{4,6},{6,4},{8,10},{10,8},{12,14},{14,12},{16,18},{18,... | collective-permute-start | bytes 24584 | tf_op jit(solution)/shard_map/ppermute | solution.py:405
  6.1 3.2 %collective-permute-start.1 = (f32[32,128]{1,0:T(8,128)S(1)}, f32[32,128]{1,0:T(8,128)S(1)}, u32[]{:S(2)}, u32[]{:S(2)}) collective-permute-start(f32[32,128]{1,0:T(8,128)S(1)} %pad_maximum_fusion.2), channel_id=1, source_target_pairs={{0,10},{2,8},{4,14},{6,12},{8,2},{10,0},{12,6},{14,4},{16,26},{18,... | collective-permute-start | bytes 49160 | tf_op jit(solution)/shard_map/ppermute | solution.py:405
  9.3 3.4 %collective-permute-start.3 = (f32[64,128]{1,0:T(8,128)S(1)}, f32[64,128]{1,0:T(8,128)S(1)}, u32[]{:S(2)}, u32[]{:S(2)}) collective-permute-start(f32[64,128]{1,0:T(8,128)S(1)} %pad_maximum_fusion.1), channel_id=1, source_target_pairs={{0,6},{2,4},{4,2},{6,0},{8,14},{10,12},{12,10},{14,8},{16,22},{18,... | collective-permute-start | bytes 98312 | tf_op jit(solution)/shard_map/ppermute | solution.py:405
  12.7 1.6 %collective-permute-start.4 = (f32[136,128]{1,0:T(8,128)S(1)}, f32[136,128]{1,0:T(8,128)S(1)}, u32[]{:S(2)}, u32[]{:S(2)}) collective-permute-start(f32[136,128]{1,0:T(8,128)S(1)} %constant_dynamic-update-slice_fusion), channel_id=1, source_target_pairs={{0,2},{2,0},{4,6},{6,4},{8,10},{10,8},{12,14},{14,12},{16,18},{18,... | collective-permute-start | bytes 208904 | tf_op jit(solution)/shard_map/ppermute | solution.py:405

commit v5 on v4

--- a/solution.py
+++ b/solution.py
@@ -82,12 +82,12 @@
 CHUNK = 16
 DEPTH = 2
 UNROLL = 8
-SIN5 = (1.5707885026931763, -0.6457120180130005, 0.07766739279031754)
+SIN5 = (2.0943219661712646, -1.5290753841400146, 0.32005560398101807)
 TOP = 1.0 / SIN5[2]
 SIN_A = SIN5[1] * TOP
 SIN_B = SIN5[0] * TOP
 TOP2 = TOP * TOP
-MU = TOP2 * TOP2 / 8.0
+MU = TOP2 * TOP / 4.0
 
 
 def pack_body(pos_ref, ang_ref, area_ref, den_ref, owner_ref, slot_ref, out_ref, need_ref):
@@ -204,9 +204,8 @@
         s = ((z + SIN_A) * z + SIN_B) * e
         q = s * s
         y = TOP2 - q
-        s = s * (y * lax.rsqrt(y))
-        c = 0.5 * TOP2 - q
-        c, s = MU - s * s, s * c
+        c = (y * lax.rsqrt(y)) * (0.25 * TOP2 - q)
+        s = s * (0.75 * TOP2 - q)
         double = facing * (inv * inv)
         b_part = double + inv * mod_b
         a_part = double * (inv * (0.5 / math.pi))
@@ -221,18 +220,25 @@
     spans = [slice(r, r + CHUNK) for r in range(top, bottom, CHUNK)]
     unroll = math.gcd(count, UNROLL * width // (bottom - top))
 
-    @pl.loop(0, count // unroll)
-    def _(group):
-        for u in range(unroll):
-            b = first_block + group * unroll + u
-            weights = load_weights(b)
-            mod_b = polar[pl.ds(b, 1), :]
-            ang_b = polar[pl.ds(blocks + b, 1), :]
-            ready = [products(weights, rows) for rows in spans[:DEPTH]]
-            for k, rows in enumerate(spans):
-                if k + DEPTH < len(spans):
-                    ready.append(products(weights, spans[k + DEPTH]))
-                add_strip(mod_b, ang_b, ready[k], rows)
+    def add_block(b):
+        weights = load_weights(b)
+        mod_b = polar[pl.ds(b, 1), :]
+        ang_b = polar[pl.ds(blocks + b, 1), :]
+        ready = [products(weights, rows) for rows in spans[:DEPTH]]
+        for k, rows in enumerate(spans):
+            if k + DEPTH < len(spans):
+                ready.append(products(weights, spans[k + DEPTH]))
+            add_strip(mod_b, ang_b, ready[k], rows)
+
+    if count == unroll:
+        for u in range(count):
+            add_block(first_block + u)
+    else:
+
+        @pl.loop(0, count // unroll)
+        def _(group):
+            for u in range(unroll):
+                add_block(first_block + group * unroll + u)
 
 
 def far_sums(acc, first, width):

time: 16.7 us -> 16.6 us (level)
  transfers between devices with their start and end apart: 5 -> 5, of which waited for: 2 -> 2; matrix products, arithmetic and copies ran while one was open for 0% -> 0% of each run, Pallas kernels for 31% -> 30%
where the time goes in v5:
time: 16.6 us; the launch traced here: 16.4 us
  Pallas kernels  7.92 us (48%)
  starting transfers between devices  7.14 us (43%)
  waiting for transfers between devices  1.29 us (8%)
    ppermute x5, starting transfers between devices, trade(): return lax.ppermute(array, 'blk', [(i, i ^ mask) for i in range(blocks)])  7.14 us
    pallas_call x4, Pallas kernels, kernel(): pl.pallas_call(body, out_shape=out_shape, in_specs=[vmem] * len(operands)...  6.09 us
    ppermute x5, waiting for transfers between devices, trade(): return lax.ppermute(array, 'blk', [(i, i ^ mask) for i in range(blocks)])  1.29 us
    pallas_call x1, Pallas kernels, on_device(): pl.pallas_call(functools.partial(own_body, panels_all), out_shape=(acc_sh...  1.06 us
    pallas_call x1, Pallas kernels, on_device(): pl.pallas_call(pack_body, out_shape=(pltpu.VMEM((ROWS * width // LANES, L...  0.77 us
  transfers between devices with their start and end apart: 5, of which 2 were waited for; matrix products, arithmetic and copies ran while one was open for 0% of the time, Pallas kernels for 30%

profile of v5, /device:TPU:0, one launch (start us, length us, event | category | flops | bytes accessed | tf_op | source)
XLA Modules:
  0.0 16.4 jit_solution(3078701856731545188)
XLA Ops:
  0.0 0.8 %pack.1 = (f32[16,128]{1,0:T(8,128)S(1)}, s32[2,256]{1,0:T(2,128)S(1)}) custom-call(f32[3,256]{1,0:T(4,128)} %pos_ref.1, f32[2,256]{1,0:T(2,128)} %ang_ref.1, f32[1,256]{1,0:T(1,128)} %bitcast.5, f32[2,256]{1,0:T(2,128)} %bitcast.4, s32[1,256]{1,0:T(1,128)} %bitcast.6, s32[1,256]{1,0:T(1,128)} %bitcast.7), custom_call_target="tpu_custom_call" | custom-call | tf_op jit(solution)/shard_map/pack/pallas_call | solution.py:387
  0.8 3.5 %collective-permute-start = (f32[16,128]{1,0:T(8,128)S(1)}, f32[16,128]{1,0:T(8,128)S(1)}, u32[]{:S(2)}, u32[]{:S(2)}) collective-permute-start(f32[16,128]{1,0:T(8,128)S(1)} %get-tuple-element.39.own_ref), channel_id=1, source_target_pairs={{0,18},{2,16},{4,22},{6,20},{8,26},{10,24},{12,30},{14,28},{16,2},... | collective-permute-start | bytes 24584 | tf_op jit(solution)/shard_map/ppermute | solution.py:411
  4.3 1.1 %far.5 = (f32[2,512,128]{2,1,0:T(8,128)S(1)}, bf16[512,24]{1,0:T(8,128)(2,1)S(1)}, s32[32,256]{1,0:T(8,128)S(1)}, f32[2,32,256]{2,1,0:T(8,128)S(1)}) custom-call(f32[16,128]{1,0:T(8,128)S(1)} %get-tuple-element.39.own_ref, s32[32,256]{1,0:T(8,128)} %index_in.1, f32[2,32,256]{2,1,0:T(8,128)} %coef_in.1), custom_call_target="tpu_custom_call" | custom-call | flops 3932160 | tf_op jit(solution)/shard_map/far/pallas_call | solution.py:439
  5.3 0.7 %collective-permute-start.2 = (f32[16,128]{1,0:T(8,128)S(1)}, f32[16,128]{1,0:T(8,128)S(1)}, u32[]{:S(2)}, u32[]{:S(2)}) collective-permute-start(f32[16,128]{1,0:T(8,128)S(1)} %get-tuple-element.39.own_ref), channel_id=1, source_target_pairs={{0,2},{2,0},{4,6},{6,4},{8,10},{10,8},{12,14},{14,12},{16,18},{18,... | collective-permute-start | bytes 24584 | tf_op jit(solution)/shard_map/ppermute | solution.py:411
  6.1 0.0 collective-permute-done.g_ref
  6.1 1.4 %collective-permute-start.1 = (f32[32,128]{1,0:T(8,128)S(1)}, f32[32,128]{1,0:T(8,128)S(1)}, u32[]{:S(2)}, u32[]{:S(2)}) collective-permute-start(f32[32,128]{1,0:T(8,128)S(1)} %pad_maximum_fusion.2), channel_id=1, source_target_pairs={{0,10},{2,8},{4,14},{6,12},{8,2},{10,0},{12,6},{14,4},{16,26},{18,... | collective-permute-start | bytes 49160 | tf_op jit(solution)/shard_map/ppermute | solution.py:411
  7.5 0.0 collective-permute-done.2.mate_ref
  7.5 1.1 %far.6 = (f32[2,512,128]{2,1,0:T(8,128)S(1)}, bf16[512,24]{1,0:T(8,128)(2,1)S(1)}) custom-call(f32[16,128]{1,0:T(8,128)S(1)} %get-tuple-element.39.own_ref, f32[16,128]{1,0:T(8,128)S(1)} %collective-permute-done.2.mate_ref, f32[16,128]{1,0:T(8,128)S(1)} %collective-permute-done.g_ref, ...), custom_call_target="tpu_custom_call", output_to_operand_aliasing={{0}: (3, {}), {1}: (4, {})} | custom-call | flops 11796480 | tf_op jit(solution)/shard_map/far/pallas_call | solution.py:415
  8.6 0.7 %collective-permute-done.1.g_ref = f32[32,128]{1,0:T(8,128)S(1)} collective-permute-done((f32[32,128]{1,0:T(8,128)S(1)}, f32[32,128]{1,0:T(8,128)S(1)}, u32[]{:S(2)}, u32[]{:S(2)}) %collective-permute-start.1) | collective-permute-done | bytes 16416 | tf_op jit(solution)/shard_map/ppermute | solution.py:411
  9.3 1.3 %collective-permute-start.3 = (f32[64,128]{1,0:T(8,128)S(1)}, f32[64,128]{1,0:T(8,128)S(1)}, u32[]{:S(2)}, u32[]{:S(2)}) collective-permute-start(f32[64,128]{1,0:T(8,128)S(1)} %pad_maximum_fusion.1), channel_id=1, source_target_pairs={{0,6},{2,4},{4,2},{6,0},{8,14},{10,12},{12,10},{14,8},{16,22},{18,... | collective-permute-start | bytes 98312 | tf_op jit(solution)/shard_map/ppermute | solution.py:411
  10.6 1.4 %far.7 = (f32[2,512,128]{2,1,0:T(8,128)S(1)}, f32[8,128]{1,0:T(8,128)S(1)}) custom-call(f32[32,128]{1,0:T(8,128)S(1)} %collective-permute-done.1.g_ref, bf16[512,24]{1,0:T(8,128)(2,1)S(1)} %get-tuple-element.47.tgt, f32[2,512,128]{2,1,0:T(8,128)S(1)} %get-tuple-element.48.acc_in), custom_call_target="tpu_custom_call", output_to_operand_aliasing={{0}: (2, {})} | custom-call | flops 15728640 | tf_op jit(solution)/shard_map/far/pallas_call | solution.py:415
  12.1 0.6 %collective-permute-done.3.g_ref = f32[64,128]{1,0:T(8,128)S(1)} collective-permute-done((f32[64,128]{1,0:T(8,128)S(1)}, f32[64,128]{1,0:T(8,128)S(1)}, u32[]{:S(2)}, u32[]{:S(2)}) %collective-permute-start.3) | collective-permute-done | bytes 32800 | tf_op jit(solution)/shard_map/ppermute | solution.py:411
  12.7 0.1 collective-permute-start.4
  12.8 1.4 %far.8.acc_in = f32[2,512,128]{2,1,0:T(8,128)S(1)} custom-call(f32[64,128]{1,0:T(8,128)S(1)} %collective-permute-done.3.g_ref, bf16[512,24]{1,0:T(8,128)(2,1)S(1)} %get-tuple-element.47.tgt, f32[2,512,128]{2,1,0:T(8,128)S(1)} %get-tuple-element.54.acc_in), custom_call_target="tpu_custom_call", output_to_operand_aliasing={{}: (2, {})} | custom-call | flops 15728640 | tf_op jit(solution)/shard_map/far/pallas_call | solution.py:415
  14.2 0.0 collective-permute-done.4.g_ref
  14.3 2.2 %far.9 = (f32[1,2,256]{2,1,0:T(2,128)}, f32[2,512,128]{2,1,0:T(8,128)S(1)}) custom-call(f32[136,128]{1,0:T(8,128)S(1)} %collective-permute-done.4.g_ref, bf16[512,24]{1,0:T(8,128)(2,1)S(1)} %get-tuple-element.47.tgt, f32[2,512,128]{2,1,0:T(8,128)S(1)} %far.8.acc_in, f32[128,128]{1,0:T(8,128)S(1)} %pad_maximum_fusion.early_ref, ...), custom_call_target="tpu_custom_call", output_to_operand_aliasing={{1}: (2, {})} | custom-call | flops 15728640 | tf_op jit(solution)/shard_map/far/pallas_call | solution.py:415
  (8 shorter events, 0.0 us)
Async XLA Ops:
  0.8 5.3 %collective-permute-start = (f32[16,128]{1,0:T(8,128)S(1)}, f32[16,128]{1,0:T(8,128)S(1)}, u32[]{:S(2)}, u32[]{:S(2)}) collective-permute-start(f32[16,128]{1,0:T(8,128)S(1)} %get-tuple-element.39.own_ref), channel_id=1, source_target_pairs={{0,18},{2,16},{4,22},{6,20},{8,26},{10,24},{12,30},{14,28},{16,2},... | collective-permute-start | bytes 24584 | tf_op jit(solution)/shard_map/ppermute | solution.py:411
  5.3 2.2 %collective-permute-start.2 = (f32[16,128]{1,0:T(8,128)S(1)}, f32[16,128]{1,0:T(8,128)S(1)}, u32[]{:S(2)}, u32[]{:S(2)}) collective-permute-start(f32[16,128]{1,0:T(8,128)S(1)} %get-tuple-element.39.own_ref), channel_id=1, source_target_pairs={{0,2},{2,0},{4,6},{6,4},{8,10},{10,8},{12,14},{14,12},{16,18},{18,... | collective-permute-start | bytes 24584 | tf_op jit(solution)/shard_map/ppermute | solution.py:411
  6.1 3.2 %collective-permute-start.1 = (f32[32,128]{1,0:T(8,128)S(1)}, f32[32,128]{1,0:T(8,128)S(1)}, u32[]{:S(2)}, u32[]{:S(2)}) collective-permute-start(f32[32,128]{1,0:T(8,128)S(1)} %pad_maximum_fusion.2), channel_id=1, source_target_pairs={{0,10},{2,8},{4,14},{6,12},{8,2},{10,0},{12,6},{14,4},{16,26},{18,... | collective-permute-start | bytes 49160 | tf_op jit(solution)/shard_map/ppermute | solution.py:411
  9.3 3.4 %collective-permute-start.3 = (f32[64,128]{1,0:T(8,128)S(1)}, f32[64,128]{1,0:T(8,128)S(1)}, u32[]{:S(2)}, u32[]{:S(2)}) collective-permute-start(f32[64,128]{1,0:T(8,128)S(1)} %pad_maximum_fusion.1), channel_id=1, source_target_pairs={{0,6},{2,4},{4,2},{6,0},{8,14},{10,12},{12,10},{14,8},{16,22},{18,... | collective-permute-start | bytes 98312 | tf_op jit(solution)/shard_map/ppermute | solution.py:411
  12.7 1.6 %collective-permute-start.4 = (f32[136,128]{1,0:T(8,128)S(1)}, f32[136,128]{1,0:T(8,128)S(1)}, u32[]{:S(2)}, u32[]{:S(2)}) collective-permute-start(f32[136,128]{1,0:T(8,128)S(1)} %constant_dynamic-update-slice_fusion), channel_id=1, source_target_pairs={{0,2},{2,0},{4,6},{6,4},{8,10},{10,8},{12,14},{14,12},{16,18},{18,... | collective-permute-start | bytes 208904 | tf_op jit(solution)/shard_map/ppermute | solution.py:411

commit v6 on v5

--- a/solution.py
+++ b/solution.py
@@ -13,6 +13,7 @@
 LANES = 128
 ROWS = 8
 KAPPA = WAVE / (2.0 * math.pi)
+TURN = 0.5 / math.pi
 
 SIN11 = (
     4.442883014678955,
@@ -208,10 +209,8 @@
         s = s * (0.75 * TOP2 - q)
         double = facing * (inv * inv)
         b_part = double + inv * mod_b
-        a_part = double * (inv * (0.5 / math.pi))
-        re = c * a_part + s * b_part
-        im = s * a_part - c * b_part
-        for part, value in ((0, re), (1, im)):
+        a_part = double * inv
+        for part, value in enumerate((c * a_part, s * b_part, s * a_part, c * b_part)):
             total = acc[part, rows, :]
             for k in range(halves):
                 total = total + value[:, k * LANES : (k + 1) * LANES]
@@ -242,16 +241,12 @@
 
 
 def far_sums(acc, first, width):
-    return [
-        jnp.concatenate(
-            [
-                jnp.sum(acc[part, h : h + LANES, :].T, 0, keepdims=True)
-                for h in range(first, first + width, LANES)
-            ],
-            1,
-        )
-        for part in range(2)
-    ]
+    sums = ([], [])
+    for h in range(first, first + width, LANES):
+        ca, sb, sa, cb = (acc[k, h : h + LANES, :] for k in range(4))
+        for part, total in enumerate((ca * TURN + sb, sa * TURN - cb)):
+            sums[part].append(jnp.sum(total.T, 0, keepdims=True))
+    return [jnp.concatenate(parts, 1) for parts in sums]
 
 
 def own_body(panels_all, own_ref, index_in, coef_in, acc, tgt, index_out, coef_out, feat, polar, sems):
@@ -424,7 +419,7 @@
             name="far",
         )(*operands)
 
-    acc_shape = pltpu.VMEM((2, 2 * width, LANES), jnp.float32)
+    acc_shape = pltpu.VMEM((4, 2 * width, LANES), jnp.float32)
     tgt_shape = pltpu.VMEM((2 * width, FEATURES), jnp.bfloat16)
     gift_shape = pltpu.VMEM((ROWS, LANES), jnp.float32)
     own = latest = held

time: 16.6 us -> 16.6 us (level)
  starting transfers between devices: 7.14 us -> 7.67 us
  waiting for transfers between devices: 1.29 us -> 0.94 us
  Pallas kernels: 7.92 us -> 7.71 us
    ppermute x5, starting transfers between devices: 7.14 us -> 7.67 us  [trade(): return lax.ppermute(array, 'blk', [(i, i ^ mask) for i in range(blocks)])]
    ppermute x5, waiting for transfers between devices: 1.29 us -> 0.94 us  [trade(): return lax.ppermute(array, 'blk', [(i, i ^ mask) for i in range(blocks)])]
    pallas_call x1, Pallas kernels: 1.06 us -> 0.88 us  [on_device(): pl.pallas_call(functools.partial(own_body, panels_all), out_shape=(acc_sh...]
  transfers between devices with their start and end apart: 5 -> 5, of which waited for: 2 -> 2; matrix products, arithmetic and copies ran while one was open for 0% -> 0% of each run, Pallas kernels for 30% -> 29%
where the time goes in v6:
time: 16.6 us; the launch traced here: 16.4 us
  Pallas kernels  7.71 us (46%)
  starting transfers between devices  7.67 us (46%)
  waiting for transfers between devices  0.94 us (6%)
    ppermute x5, starting transfers between devices, trade(): return lax.ppermute(array, 'blk', [(i, i ^ mask) for i in range(blocks)])  7.67 us
    pallas_call x4, Pallas kernels, kernel(): pl.pallas_call(body, out_shape=out_shape, in_specs=[vmem] * len(operands)...  6.07 us
    ppermute x5, waiting for transfers between devices, trade(): return lax.ppermute(array, 'blk', [(i, i ^ mask) for i in range(blocks)])  0.94 us
    pallas_call x1, Pallas kernels, on_device(): pl.pallas_call(functools.partial(own_body, panels_all), out_shape=(acc_sh...  0.88 us
    pallas_call x1, Pallas kernels, on_device(): pl.pallas_call(pack_body, out_shape=(pltpu.VMEM((ROWS * width // LANES, L...  0.77 us
  transfers between devices with their start and end apart: 5, of which 2 were waited for; matrix products, arithmetic and copies ran while one was open for 0% of the time, Pallas kernels for 29%

profile of v6, /device:TPU:0, one launch (start us, length us, event | category | flops | bytes accessed | tf_op | source)
XLA Modules:
  0.0 16.4 jit_solution(12150715760156596752)
XLA Ops:
  0.0 0.8 %pack.1 = (f32[16,128]{1,0:T(8,128)S(1)}, s32[2,256]{1,0:T(2,128)S(1)}) custom-call(f32[3,256]{1,0:T(4,128)} %pos_ref.1, f32[2,256]{1,0:T(2,128)} %ang_ref.1, f32[1,256]{1,0:T(1,128)} %bitcast.5, f32[2,256]{1,0:T(2,128)} %bitcast.4, s32[1,256]{1,0:T(1,128)} %bitcast.6, s32[1,256]{1,0:T(1,128)} %bitcast.7), custom_call_target="tpu_custom_call" | custom-call | tf_op jit(solution)/shard_map/pack/pallas_call | solution.py:382
  0.8 3.5 %collective-permute-start = (f32[16,128]{1,0:T(8,128)S(1)}, f32[16,128]{1,0:T(8,128)S(1)}, u32[]{:S(2)}, u32[]{:S(2)}) collective-permute-start(f32[16,128]{1,0:T(8,128)S(1)} %get-tuple-element.39.own_ref), channel_id=1, source_target_pairs={{0,18},{2,16},{4,22},{6,20},{8,26},{10,24},{12,30},{14,28},{16,2},... | collective-permute-start | bytes 24584 | tf_op jit(solution)/shard_map/ppermute | solution.py:406
  4.3 0.9 %far.5 = (f32[4,512,128]{2,1,0:T(8,128)S(1)}, bf16[512,24]{1,0:T(8,128)(2,1)S(1)}, s32[32,256]{1,0:T(8,128)S(1)}, f32[2,32,256]{2,1,0:T(8,128)S(1)}) custom-call(f32[16,128]{1,0:T(8,128)S(1)} %get-tuple-element.39.own_ref, s32[32,256]{1,0:T(8,128)} %index_in.1, f32[2,32,256]{2,1,0:T(8,128)} %coef_in.1), custom_call_target="tpu_custom_call" | custom-call | flops 3932160 | tf_op jit(solution)/shard_map/far/pallas_call | solution.py:434
  5.2 0.7 %collective-permute-start.2 = (f32[16,128]{1,0:T(8,128)S(1)}, f32[16,128]{1,0:T(8,128)S(1)}, u32[]{:S(2)}, u32[]{:S(2)}) collective-permute-start(f32[16,128]{1,0:T(8,128)S(1)} %get-tuple-element.39.own_ref), channel_id=1, source_target_pairs={{0,2},{2,0},{4,6},{6,4},{8,10},{10,8},{12,14},{14,12},{16,18},{18,... | collective-permute-start | bytes 24584 | tf_op jit(solution)/shard_map/ppermute | solution.py:406
  5.9 0.0 collective-permute-done.g_ref
  5.9 1.6 %collective-permute-start.1 = (f32[32,128]{1,0:T(8,128)S(1)}, f32[32,128]{1,0:T(8,128)S(1)}, u32[]{:S(2)}, u32[]{:S(2)}) collective-permute-start(f32[32,128]{1,0:T(8,128)S(1)} %pad_maximum_fusion.2), channel_id=1, source_target_pairs={{0,10},{2,8},{4,14},{6,12},{8,2},{10,0},{12,6},{14,4},{16,26},{18,... | collective-permute-start | bytes 49160 | tf_op jit(solution)/shard_map/ppermute | solution.py:406
  7.5 0.0 collective-permute-done.2.mate_ref
  7.5 1.1 %far.6 = (f32[4,512,128]{2,1,0:T(8,128)S(1)}, bf16[512,24]{1,0:T(8,128)(2,1)S(1)}) custom-call(f32[16,128]{1,0:T(8,128)S(1)} %get-tuple-element.39.own_ref, f32[16,128]{1,0:T(8,128)S(1)} %collective-permute-done.2.mate_ref, f32[16,128]{1,0:T(8,128)S(1)} %collective-permute-done.g_ref, ...), custom_call_target="tpu_custom_call", output_to_operand_aliasing={{0}: (3, {}), {1}: (4, {})} | custom-call | flops 11796480 | tf_op jit(solution)/shard_map/far/pallas_call | solution.py:410
  8.6 0.5 %collective-permute-done.1.g_ref = f32[32,128]{1,0:T(8,128)S(1)} collective-permute-done((f32[32,128]{1,0:T(8,128)S(1)}, f32[32,128]{1,0:T(8,128)S(1)}, u32[]{:S(2)}, u32[]{:S(2)}) %collective-permute-start.1) | collective-permute-done | bytes 16416 | tf_op jit(solution)/shard_map/ppermute | solution.py:406
  9.1 1.5 %collective-permute-start.3 = (f32[64,128]{1,0:T(8,128)S(1)}, f32[64,128]{1,0:T(8,128)S(1)}, u32[]{:S(2)}, u32[]{:S(2)}) collective-permute-start(f32[64,128]{1,0:T(8,128)S(1)} %pad_maximum_fusion.1), channel_id=1, source_target_pairs={{0,6},{2,4},{4,2},{6,0},{8,14},{10,12},{12,10},{14,8},{16,22},{18,... | collective-permute-start | bytes 98312 | tf_op jit(solution)/shard_map/ppermute | solution.py:406
  10.6 1.4 %far.7 = (f32[4,512,128]{2,1,0:T(8,128)S(1)}, f32[8,128]{1,0:T(8,128)S(1)}) custom-call(f32[32,128]{1,0:T(8,128)S(1)} %collective-permute-done.1.g_ref, bf16[512,24]{1,0:T(8,128)(2,1)S(1)} %get-tuple-element.47.tgt, f32[4,512,128]{2,1,0:T(8,128)S(1)} %get-tuple-element.48.acc_in), custom_call_target="tpu_custom_call", output_to_operand_aliasing={{0}: (2, {})} | custom-call | flops 15728640 | tf_op jit(solution)/shard_map/far/pallas_call | solution.py:410
  12.1 0.4 %collective-permute-done.3.g_ref = f32[64,128]{1,0:T(8,128)S(1)} collective-permute-done((f32[64,128]{1,0:T(8,128)S(1)}, f32[64,128]{1,0:T(8,128)S(1)}, u32[]{:S(2)}, u32[]{:S(2)}) %collective-permute-start.3) | collective-permute-done | bytes 32800 | tf_op jit(solution)/shard_map/ppermute | solution.py:406
  12.5 0.3 %collective-permute-start.4 = (f32[136,128]{1,0:T(8,128)S(1)}, f32[136,128]{1,0:T(8,128)S(1)}, u32[]{:S(2)}, u32[]{:S(2)}) collective-permute-start(f32[136,128]{1,0:T(8,128)S(1)} %constant_dynamic-update-slice_fusion), channel_id=1, source_target_pairs={{0,2},{2,0},{4,6},{6,4},{8,10},{10,8},{12,14},{14,12},{16,18},{18,... | collective-permute-start | bytes 208904 | tf_op jit(solution)/shard_map/ppermute | solution.py:406
  12.8 1.4 %far.8.acc_in = f32[4,512,128]{2,1,0:T(8,128)S(1)} custom-call(f32[64,128]{1,0:T(8,128)S(1)} %collective-permute-done.3.g_ref, bf16[512,24]{1,0:T(8,128)(2,1)S(1)} %get-tuple-element.47.tgt, f32[4,512,128]{2,1,0:T(8,128)S(1)} %get-tuple-element.54.acc_in), custom_call_target="tpu_custom_call", output_to_operand_aliasing={{}: (2, {})} | custom-call | flops 15728640 | tf_op jit(solution)/shard_map/far/pallas_call | solution.py:410
  14.2 0.0 collective-permute-done.4.g_ref
  14.2 2.2 %far.9 = (f32[1,2,256]{2,1,0:T(2,128)}, f32[4,512,128]{2,1,0:T(8,128)S(1)}) custom-call(f32[136,128]{1,0:T(8,128)S(1)} %collective-permute-done.4.g_ref, bf16[512,24]{1,0:T(8,128)(2,1)S(1)} %get-tuple-element.47.tgt, f32[4,512,128]{2,1,0:T(8,128)S(1)} %far.8.acc_in, f32[128,128]{1,0:T(8,128)S(1)} %pad_maximum_fusion.early_ref, ...), custom_call_target="tpu_custom_call", output_to_operand_aliasing={{1}: (2, {})} | custom-call | flops 15728640 | tf_op jit(solution)/shard_map/far/pallas_call | solution.py:410
  (8 shorter events, 0.0 us)
Async XLA Ops:
  0.8 5.1 %collective-permute-start = (f32[16,128]{1,0:T(8,128)S(1)}, f32[16,128]{1,0:T(8,128)S(1)}, u32[]{:S(2)}, u32[]{:S(2)}) collective-permute-start(f32[16,128]{1,0:T(8,128)S(1)} %get-tuple-element.39.own_ref), channel_id=1, source_target_pairs={{0,18},{2,16},{4,22},{6,20},{8,26},{10,24},{12,30},{14,28},{16,2},... | collective-permute-start | bytes 24584 | tf_op jit(solution)/shard_map/ppermute | solution.py:406
  5.2 2.4 %collective-permute-start.2 = (f32[16,128]{1,0:T(8,128)S(1)}, f32[16,128]{1,0:T(8,128)S(1)}, u32[]{:S(2)}, u32[]{:S(2)}) collective-permute-start(f32[16,128]{1,0:T(8,128)S(1)} %get-tuple-element.39.own_ref), channel_id=1, source_target_pairs={{0,2},{2,0},{4,6},{6,4},{8,10},{10,8},{12,14},{14,12},{16,18},{18,... | collective-permute-start | bytes 24584 | tf_op jit(solution)/shard_map/ppermute | solution.py:406
  5.9 3.2 %collective-permute-start.1 = (f32[32,128]{1,0:T(8,128)S(1)}, f32[32,128]{1,0:T(8,128)S(1)}, u32[]{:S(2)}, u32[]{:S(2)}) collective-permute-start(f32[32,128]{1,0:T(8,128)S(1)} %pad_maximum_fusion.2), channel_id=1, source_target_pairs={{0,10},{2,8},{4,14},{6,12},{8,2},{10,0},{12,6},{14,4},{16,26},{18,... | collective-permute-start | bytes 49160 | tf_op jit(solution)/shard_map/ppermute | solution.py:406
  9.1 3.3 %collective-permute-start.3 = (f32[64,128]{1,0:T(8,128)S(1)}, f32[64,128]{1,0:T(8,128)S(1)}, u32[]{:S(2)}, u32[]{:S(2)}) collective-permute-start(f32[64,128]{1,0:T(8,128)S(1)} %pad_maximum_fusion.1), channel_id=1, source_target_pairs={{0,6},{2,4},{4,2},{6,0},{8,14},{10,12},{12,10},{14,8},{16,22},{18,... | collective-permute-start | bytes 98312 | tf_op jit(solution)/shard_map/ppermute | solution.py:406
  12.5 1.7 %collective-permute-start.4 = (f32[136,128]{1,0:T(8,128)S(1)}, f32[136,128]{1,0:T(8,128)S(1)}, u32[]{:S(2)}, u32[]{:S(2)}) collective-permute-start(f32[136,128]{1,0:T(8,128)S(1)} %constant_dynamic-update-slice_fusion), channel_id=1, source_target_pairs={{0,2},{2,0},{4,6},{6,4},{8,10},{10,8},{12,14},{14,12},{16,18},{18,... | collective-permute-start | bytes 208904 | tf_op jit(solution)/shard_map/ppermute | solution.py:406

commit v7 on v5

--- a/solution.py
+++ b/solution.py
@@ -176,7 +176,7 @@
     tgt[first : first + width, :] = stacked.T.astype(jnp.bfloat16)
 
 
-def add_far(feat, polar, tgt, acc, first_block, count, top, bottom):
+def add_far(feat, polar, tgt, acc, first_block, count, top, bottom, side=None):
     blocks, width = polar.shape[0] // 2, polar.shape[1]
     halves = width // LANES
 
@@ -229,6 +229,8 @@
             if k + DEPTH < len(spans):
                 ready.append(products(weights, spans[k + DEPTH]))
             add_strip(mod_b, ang_b, ready[k], rows)
+            if side is not None and count == unroll:
+                next(side, None)
 
     if count == unroll:
         for u in range(count):
@@ -300,66 +302,91 @@
 
 
 def last_body(
-    panels_all, masks, g_ref, tgt, acc_in, early_ref, need_ref, index_ref, coef_ref, out_ref, acc, feat, polar
+    panels_all, masks, g_ref, tgt, acc_in, early_ref, need_ref, index_ref, coef_ref, out_ref, feat, polar, acc
 ):
     width = need_ref.shape[1]
     halves = width // LANES
     me = lax.axis_index("blk")
     fresh = polar.shape[0] // 2
     held = 2 * fresh
+    acc[...] = acc_in[:, :width, :]
+    blocks = 2 * held
     source_features(panels_all, [(g_ref, fresh, fresh)], feat, polar)
-    add_far(feat, polar, tgt, acc, 0, fresh, 0, width)
-    far = far_sums(acc, 0, width)
-
-    owner = need_ref[0:1, :]
-    slot = need_ref[1:2, :]
-    blocks = 2 * held
-    den = []
-    for k in (6, 7):
-        den.append(take_row([(early_ref, 0, held), (g_ref, 0, held)], halves, k))
-    need = []
+    result = []
+
+    def near_field():
+        owner = need_ref[0:1, :]
+        slot = need_ref[1:2, :]
+        den = []
+        for k in (6, 7):
+            den.append(take_row([(early_ref, 0, held), (g_ref, 0, held)], halves, k))
+        need = []
+        for h in range(halves):
+            lanes = slice(h * LANES, (h + 1) * LANES)
+            slot_h = jnp.broadcast_to(slot[:, lanes], (ROWS, LANES))
+            own_h = jnp.broadcast_to(owner[:, lanes], (ROWS, LANES))
+            sums = [jnp.zeros((ROWS, LANES), jnp.float32)] * 2
+            for p in range(0, blocks, ROWS):
+                place = lax.broadcasted_iota(jnp.int32, (ROWS, LANES), 0) + p
+                device = me
+                for k, mask in enumerate(masks):
+                    device = device ^ (((place >> k) & 1) * mask)
+                mine = own_h == device
+                for part in range(2):
+                    for k in range(halves):
+                        got = jnp.take_along_axis(
+                            den[part][p : p + ROWS, k * LANES : (k + 1) * LANES], slot_h % LANES, axis=1
+                        )
+                        sums[part] = sums[part] + jnp.where(mine & (slot_h // LANES == k), got, 0.0)
+                    yield
+            need.append([jnp.broadcast_to(jnp.sum(v, 0, keepdims=True), (ROWS, LANES)) for v in sums])
+
+        count = index_ref.shape[0]
+        for h in range(halves):
+            lanes = slice(h * LANES, (h + 1) * LANES)
+            near = [jnp.zeros((ROWS, LANES), jnp.float32)] * 2
+            for m in range(0, count, ROWS):
+                where = index_ref[m : m + ROWS, lanes]
+                picked = []
+                for part in range(2):
+                    got = jnp.zeros((ROWS, LANES), jnp.float32)
+                    for k in range(halves):
+                        one_half = jnp.take_along_axis(need[k][part], where % LANES, axis=1)
+                        got = jnp.where(where // LANES == k, one_half, got)
+                    picked.append(got)
+                    yield
+                cr = coef_ref[0, m : m + ROWS, lanes]
+                ci = coef_ref[1, m : m + ROWS, lanes]
+                near[0] = near[0] + (cr * picked[0] - ci * picked[1])
+                near[1] = near[1] + (cr * picked[1] + ci * picked[0])
+            result.append([jnp.sum(v, 0, keepdims=True) for v in near])
+            yield
+
+    far = []
+
+    def side_work():
+        laid = 0
+        for _ in near_field():
+            laid += 1
+            yield
+        for _ in range(laid, ((fresh - 1) * width + LANES) // CHUNK):
+            yield
+        far.append(far_sums(acc, 0, LANES))
+        yield
+
+    side = side_work()
+    add_far(feat, polar, tgt, acc, 0, fresh, 0, width, side)
+    for _ in side:
+        pass
+    far += [far_sums(acc, h * LANES, LANES) for h in range(1, halves)]
     for h in range(halves):
         lanes = slice(h * LANES, (h + 1) * LANES)
-        slot_h = jnp.broadcast_to(slot[:, lanes], (ROWS, LANES))
-        own_h = jnp.broadcast_to(owner[:, lanes], (ROWS, LANES))
-        sums = [jnp.zeros((ROWS, LANES), jnp.float32)] * 2
-        for p in range(0, blocks, ROWS):
-            place = lax.broadcasted_iota(jnp.int32, (ROWS, LANES), 0) + p
-            device = me
-            for k, mask in enumerate(masks):
-                device = device ^ (((place >> k) & 1) * mask)
-            mine = own_h == device
-            for part in range(2):
-                for k in range(halves):
-                    got = jnp.take_along_axis(
-                        den[part][p : p + ROWS, k * LANES : (k + 1) * LANES], slot_h % LANES, axis=1
-                    )
-                    sums[part] = sums[part] + jnp.where(mine & (slot_h // LANES == k), got, 0.0)
-        need.append([jnp.broadcast_to(jnp.sum(v, 0, keepdims=True), (ROWS, LANES)) for v in sums])
-
-    count = index_ref.shape[0]
-    for h in range(halves):
-        lanes = slice(h * LANES, (h + 1) * LANES)
-        near = [jnp.zeros((ROWS, LANES), jnp.float32)] * 2
-        for m in range(0, count, ROWS):
-            where = index_ref[m : m + ROWS, lanes]
-            picked = []
-            for part in range(2):
-                got = jnp.zeros((ROWS, LANES), jnp.float32)
-                for k in range(halves):
-                    one_half = jnp.take_along_axis(need[k][part], where % LANES, axis=1)
-                    got = jnp.where(where // LANES == k, one_half, got)
-                picked.append(got)
-            cr = coef_ref[0, m : m + ROWS, lanes]
-            ci = coef_ref[1, m : m + ROWS, lanes]
-            near[0] = near[0] + (cr * picked[0] - ci * picked[1])
-            near[1] = near[1] + (cr * picked[1] + ci * picked[0])
         for part in range(2):
             own = early_ref[h * ROWS + 6 + part : h * ROWS + 7 + part, :]
             k = blocks * halves * ROWS // 2 + part * halves + h
             gift = g_ref[k : k + 1, :]
             out_ref[0, part : part + 1, lanes] = (
-                0.5 * own + (far[part][:, lanes] + gift) + jnp.sum(near[part], 0, keepdims=True)
+                0.5 * own + (far[h][part] + gift) + result[h][part]
             )
 
 
@@ -486,15 +513,16 @@
         latest = arrived
         held = jnp.concatenate([held, arrived], 0)
         count *= 2
-    out = kernel(
+    return pl.pallas_call(
         functools.partial(last_body, panels_all, tuple(masks)),
-        (jax.ShapeDtypeStruct(densities.shape, jnp.float32), acc_shape),
-        (latest, tgt, acc, early, need, index, coef),
-        count // 4,
-        count // 4,
-        {2: 1},
-    )
-    return out[0]
+        out_shape=jax.ShapeDtypeStruct(densities.shape, jnp.float32),
+        in_specs=[vmem] * 7,
+        out_specs=vmem,
+        scratch_shapes=scratch(count // 4, width) + [pltpu.VMEM((2, width, LANES), jnp.float32)],
+        compiler_params=params,
+        cost_estimate=far_cost(count // 4, width),
+        name="last",
+    )(latest, tgt, acc, early, need, index, coef)
 
 
 def solution(mesh):

time: 16.6 us -> 16.5 us (level)
    pallas_call x4 -> x3, Pallas kernels: 6.09 us -> 3.93 us  [kernel(): pl.pallas_call(body, out_shape=out_shape, in_specs=[vmem] * len(operands)...]
    pallas_call x0 -> x1, Pallas kernels: none -> 2.09 us  [on_device(): pl.pallas_call(functools.partial(last_body, panels_all, tuple(masks)), ou...]
  transfers between devices with their start and end apart: 5 -> 5, of which waited for: 2 -> 2; matrix products, arithmetic and copies ran while one was open for 0% -> 0% of each run, Pallas kernels for 30% -> 31%
where the time goes in v7:
time: 16.5 us; the launch traced here: 16.3 us
  Pallas kernels  7.85 us (48%)
  starting transfers between devices  7.14 us (43%)
  waiting for transfers between devices  1.29 us (8%)
    ppermute x5, starting transfers between devices, trade(): return lax.ppermute(array, 'blk', [(i, i ^ mask) for i in range(blocks)])  7.14 us
    pallas_call x3, Pallas kernels, kernel(): pl.pallas_call(body, out_shape=out_shape, in_specs=[vmem] * len(operands)...  3.93 us
    pallas_call x1, Pallas kernels, on_device(): pl.pallas_call(functools.partial(last_body, panels_all, tuple(masks)), ou...  2.09 us
    ppermute x5, waiting for transfers between devices, trade(): return lax.ppermute(array, 'blk', [(i, i ^ mask) for i in range(blocks)])  1.29 us
    pallas_call x1, Pallas kernels, on_device(): pl.pallas_call(functools.partial(own_body, panels_all), out_shape=(acc_sh...  1.06 us
    pallas_call x1, Pallas kernels, on_device(): pl.pallas_call(pack_body, out_shape=(pltpu.VMEM((ROWS * width // LANES, L...  0.77 us
  transfers between devices with their start and end apart: 5, of which 2 were waited for; matrix products, arithmetic and copies ran while one was open for 0% of the time, Pallas kernels for 31%

profile of v7, /device:TPU:0, one launch (start us, length us, event | category | flops | bytes accessed | tf_op | source)
XLA Modules:
  0.0 16.3 jit_solution(12567722587506994656)
XLA Ops:
  0.0 0.8 %pack.1 = (f32[16,128]{1,0:T(8,128)S(1)}, s32[2,256]{1,0:T(2,128)S(1)}) custom-call(f32[3,256]{1,0:T(4,128)} %pos_ref.1, f32[2,256]{1,0:T(2,128)} %ang_ref.1, f32[1,256]{1,0:T(1,128)} %bitcast.5, f32[2,256]{1,0:T(2,128)} %bitcast.4, s32[1,256]{1,0:T(1,128)} %bitcast.6, s32[1,256]{1,0:T(1,128)} %bitcast.7), custom_call_target="tpu_custom_call" | custom-call | tf_op jit(solution)/shard_map/pack/pallas_call | solution.py:414
  0.8 3.5 %collective-permute-start = (f32[16,128]{1,0:T(8,128)S(1)}, f32[16,128]{1,0:T(8,128)S(1)}, u32[]{:S(2)}, u32[]{:S(2)}) collective-permute-start(f32[16,128]{1,0:T(8,128)S(1)} %get-tuple-element.38.own_ref), channel_id=1, source_target_pairs={{0,18},{2,16},{4,22},{6,20},{8,26},{10,24},{12,30},{14,28},{16,2},... | collective-permute-start | bytes 24584 | tf_op jit(solution)/shard_map/ppermute | solution.py:438
  4.3 1.1 %far.4 = (f32[2,512,128]{2,1,0:T(8,128)S(1)}, bf16[512,24]{1,0:T(8,128)(2,1)S(1)}, s32[32,256]{1,0:T(8,128)S(1)}, f32[2,32,256]{2,1,0:T(8,128)S(1)}) custom-call(f32[16,128]{1,0:T(8,128)S(1)} %get-tuple-element.38.own_ref, s32[32,256]{1,0:T(8,128)} %index_in.1, f32[2,32,256]{2,1,0:T(8,128)} %coef_in.1), custom_call_target="tpu_custom_call" | custom-call | flops 3932160 | tf_op jit(solution)/shard_map/far/pallas_call | solution.py:466
  5.3 0.7 %collective-permute-start.2 = (f32[16,128]{1,0:T(8,128)S(1)}, f32[16,128]{1,0:T(8,128)S(1)}, u32[]{:S(2)}, u32[]{:S(2)}) collective-permute-start(f32[16,128]{1,0:T(8,128)S(1)} %get-tuple-element.38.own_ref), channel_id=1, source_target_pairs={{0,2},{2,0},{4,6},{6,4},{8,10},{10,8},{12,14},{14,12},{16,18},{18,... | collective-permute-start | bytes 24584 | tf_op jit(solution)/shard_map/ppermute | solution.py:438
  6.1 0.0 collective-permute-done.g_ref
  6.1 1.4 %collective-permute-start.1 = (f32[32,128]{1,0:T(8,128)S(1)}, f32[32,128]{1,0:T(8,128)S(1)}, u32[]{:S(2)}, u32[]{:S(2)}) collective-permute-start(f32[32,128]{1,0:T(8,128)S(1)} %pad_maximum_fusion.2), channel_id=1, source_target_pairs={{0,10},{2,8},{4,14},{6,12},{8,2},{10,0},{12,6},{14,4},{16,26},{18,... | collective-permute-start | bytes 49160 | tf_op jit(solution)/shard_map/ppermute | solution.py:438
  7.5 0.0 collective-permute-done.2.mate_ref
  7.5 1.1 %far.5 = (f32[2,512,128]{2,1,0:T(8,128)S(1)}, bf16[512,24]{1,0:T(8,128)(2,1)S(1)}) custom-call(f32[16,128]{1,0:T(8,128)S(1)} %get-tuple-element.38.own_ref, f32[16,128]{1,0:T(8,128)S(1)} %collective-permute-done.2.mate_ref, f32[16,128]{1,0:T(8,128)S(1)} %collective-permute-done.g_ref, ...), custom_call_target="tpu_custom_call", output_to_operand_aliasing={{0}: (3, {}), {1}: (4, {})} | custom-call | flops 11796480 | tf_op jit(solution)/shard_map/far/pallas_call | solution.py:442
  8.6 0.7 %collective-permute-done.1.g_ref = f32[32,128]{1,0:T(8,128)S(1)} collective-permute-done((f32[32,128]{1,0:T(8,128)S(1)}, f32[32,128]{1,0:T(8,128)S(1)}, u32[]{:S(2)}, u32[]{:S(2)}) %collective-permute-start.1) | collective-permute-done | bytes 16416 | tf_op jit(solution)/shard_map/ppermute | solution.py:438
  9.3 1.3 %collective-permute-start.3 = (f32[64,128]{1,0:T(8,128)S(1)}, f32[64,128]{1,0:T(8,128)S(1)}, u32[]{:S(2)}, u32[]{:S(2)}) collective-permute-start(f32[64,128]{1,0:T(8,128)S(1)} %pad_maximum_fusion.1), channel_id=1, source_target_pairs={{0,6},{2,4},{4,2},{6,0},{8,14},{10,12},{12,10},{14,8},{16,22},{18,... | collective-permute-start | bytes 98312 | tf_op jit(solution)/shard_map/ppermute | solution.py:438
  10.6 1.4 %far.6 = (f32[2,512,128]{2,1,0:T(8,128)S(1)}, f32[8,128]{1,0:T(8,128)S(1)}) custom-call(f32[32,128]{1,0:T(8,128)S(1)} %collective-permute-done.1.g_ref, bf16[512,24]{1,0:T(8,128)(2,1)S(1)} %get-tuple-element.46.tgt, f32[2,512,128]{2,1,0:T(8,128)S(1)} %get-tuple-element.47.acc_in), custom_call_target="tpu_custom_call", output_to_operand_aliasing={{0}: (2, {})} | custom-call | flops 15728640 | tf_op jit(solution)/shard_map/far/pallas_call | solution.py:442
  12.1 0.6 %collective-permute-done.3.g_ref = f32[64,128]{1,0:T(8,128)S(1)} collective-permute-done((f32[64,128]{1,0:T(8,128)S(1)}, f32[64,128]{1,0:T(8,128)S(1)}, u32[]{:S(2)}, u32[]{:S(2)}) %collective-permute-start.3) | collective-permute-done | bytes 32800 | tf_op jit(solution)/shard_map/ppermute | solution.py:438
  12.7 0.1 collective-permute-start.4
  12.8 1.4 %far.7.acc_in = f32[2,512,128]{2,1,0:T(8,128)S(1)} custom-call(f32[64,128]{1,0:T(8,128)S(1)} %collective-permute-done.3.g_ref, bf16[512,24]{1,0:T(8,128)(2,1)S(1)} %get-tuple-element.46.tgt, f32[2,512,128]{2,1,0:T(8,128)S(1)} %get-tuple-element.53.acc_in), custom_call_target="tpu_custom_call", output_to_operand_aliasing={{}: (2, {})} | custom-call | flops 15728640 | tf_op jit(solution)/shard_map/far/pallas_call | solution.py:442
  14.2 0.0 collective-permute-done.4.g_ref
  14.3 2.1 %last.1 = f32[1,2,256]{2,1,0:T(2,128)} custom-call(f32[136,128]{1,0:T(8,128)S(1)} %collective-permute-done.4.g_ref, bf16[512,24]{1,0:T(8,128)(2,1)S(1)} %get-tuple-element.46.tgt, f32[2,512,128]{2,1,0:T(8,128)S(1)} %far.7.acc_in, f32[128,128]{1,0:T(8,128)S(1)} %pad_maximum_fusion.early_ref, s32[2,256]{1,0:T(2,128)S(1)} %get-tuple-element.56.need_ref, ...), custom_call_target="tpu_custom_call" | custom-call | flops 15728640 | tf_op jit(solution)/shard_map/last/pallas_call | solution.py:516
  (8 shorter events, 0.0 us)
Async XLA Ops:
  0.8 5.3 %collective-permute-start = (f32[16,128]{1,0:T(8,128)S(1)}, f32[16,128]{1,0:T(8,128)S(1)}, u32[]{:S(2)}, u32[]{:S(2)}) collective-permute-start(f32[16,128]{1,0:T(8,128)S(1)} %get-tuple-element.38.own_ref), channel_id=1, source_target_pairs={{0,18},{2,16},{4,22},{6,20},{8,26},{10,24},{12,30},{14,28},{16,2},... | collective-permute-start | bytes 24584 | tf_op jit(solution)/shard_map/ppermute | solution.py:438
  5.3 2.2 %collective-permute-start.2 = (f32[16,128]{1,0:T(8,128)S(1)}, f32[16,128]{1,0:T(8,128)S(1)}, u32[]{:S(2)}, u32[]{:S(2)}) collective-permute-start(f32[16,128]{1,0:T(8,128)S(1)} %get-tuple-element.38.own_ref), channel_id=1, source_target_pairs={{0,2},{2,0},{4,6},{6,4},{8,10},{10,8},{12,14},{14,12},{16,18},{18,... | collective-permute-start | bytes 24584 | tf_op jit(solution)/shard_map/ppermute | solution.py:438
  6.1 3.2 %collective-permute-start.1 = (f32[32,128]{1,0:T(8,128)S(1)}, f32[32,128]{1,0:T(8,128)S(1)}, u32[]{:S(2)}, u32[]{:S(2)}) collective-permute-start(f32[32,128]{1,0:T(8,128)S(1)} %pad_maximum_fusion.2), channel_id=1, source_target_pairs={{0,10},{2,8},{4,14},{6,12},{8,2},{10,0},{12,6},{14,4},{16,26},{18,... | collective-permute-start | bytes 49160 | tf_op jit(solution)/shard_map/ppermute | solution.py:438
  9.3 3.4 %collective-permute-start.3 = (f32[64,128]{1,0:T(8,128)S(1)}, f32[64,128]{1,0:T(8,128)S(1)}, u32[]{:S(2)}, u32[]{:S(2)}) collective-permute-start(f32[64,128]{1,0:T(8,128)S(1)} %pad_maximum_fusion.1), channel_id=1, source_target_pairs={{0,6},{2,4},{4,2},{6,0},{8,14},{10,12},{12,10},{14,8},{16,22},{18,... | collective-permute-start | bytes 98312 | tf_op jit(solution)/shard_map/ppermute | solution.py:438
  12.7 1.6 %collective-permute-start.4 = (f32[136,128]{1,0:T(8,128)S(1)}, f32[136,128]{1,0:T(8,128)S(1)}, u32[]{:S(2)}, u32[]{:S(2)}) collective-permute-start(f32[136,128]{1,0:T(8,128)S(1)} %constant_dynamic-update-slice_fusion), channel_id=1, source_target_pairs={{0,2},{2,0},{4,6},{6,4},{8,10},{10,8},{12,14},{14,12},{16,18},{18,... | collective-permute-start | bytes 208904 | tf_op jit(solution)/shard_map/ppermute | solution.py:438
